TPU v7x, 512 devices: a whole 4x8x8 slice. The times are simulated.
512 devices in a mesh: tm: 8 (over y), rows: 8 (over z_lo, core), cols: 8 (over z_hi, x).
Axes of the slice: x: 4, y: 8, z: 8 (z_hi: 2, z_lo: 4; z = z_hi * 4 + z_lo), core: 2. Of those that a mesh axis runs over, the one named last changes fastest.
Arguments:
- latent: bfloat16 [24, 16, 64, 384], P('tm', 'rows', 'cols'), may hold values from -6 to 6
- cotangent: bfloat16 [24, 32, 128, 192], P('tm', 'rows', 'cols'), may hold values from -6 to 6
- resample_weight: bfloat16 [3, 3, 384, 192], replicated, may hold values from -0.109375 to 0.109375
- conv_weight: bfloat16 [3, 3, 3, 192, 192], replicated, may hold values from -0.078125 to 0.078125
- norm_gain: float32 [192], replicated, may hold values from 0.1 to 1.9
Outputs:
- grad_input: bfloat16 [24, 16, 64, 384], P('tm', 'rows', 'cols')
- grad_resample: float32 [663552], P(('tm', 'rows', 'cols'))
- grad_conv: float32 [995328], P(('tm', 'rows', 'cols'))
- grad_gain: float32 [192], replicated
All inputs are finite; a program needn't handle non-finite values.
Results may differ from a plain program's by a relative error of at most 0.013.
Values may be sent and summed in bfloat16 or wider, within the bound.
A program may use at most 128 MiB of HBM per device.

v0:
```python
import jax
import jax.numpy as jnp
from jax import lax
from jax.sharding import PartitionSpec as P

EPSILON = 1e-06


def with_halo(x, sides, width):
    for axis, dim in sides:
        count, length = (lax.axis_size(axis), x.shape[dim])
        up = [(i, (i + 1) % count) for i in range(count - 1)]
        down = [(j, i) for i, j in up]
        last = lax.slice_in_dim(x, length - width, length, axis=dim)
        first = lax.slice_in_dim(x, 0, width, axis=dim)
        before = lax.ppermute(last, axis, up)
        after = lax.ppermute(first, axis, down)
        x = jnp.concatenate([before, x, after], axis=dim)
    return x


def from_behind(x, axis, by):
    count = lax.axis_size(axis)
    pairs = [(i, i + by) for i in range(count) if 0 <= i + by < count]
    return lax.ppermute(x, axis, pairs)


def upsample(values):
    return jnp.repeat(jnp.repeat(values, 2, axis=1), 2, axis=2)


def taps_plane(source, height, width):
    return jnp.concatenate(
        [
            source[:, step_y : step_y + height, step_x : step_x + width]
            for step_y in range(3)
            for step_x in range(3)
        ],
        axis=-1,
    )


def taps_volume(source, frames, height, width):
    return jnp.concatenate(
        [
            source[step_t : step_t + frames, step_y : step_y + height, step_x : step_x + width]
            for step_t in range(3)
            for step_y in range(3)
            for step_x in range(3)
        ],
        axis=-1,
    )


def statistics(z_float, gain):
    inverse = lax.rsqrt(jnp.mean(z_float * z_float, axis=-1, keepdims=True) + EPSILON)
    normed = z_float * inverse
    scaled = normed * gain
    sigma = jax.nn.sigmoid(scaled)
    return (inverse, normed, scaled, sigma, (scaled * sigma).astype(jnp.bfloat16))


def contract_rows(left, right):
    return lax.dot_general(
        left, right, (((0,), (0,)), ((), ())), preferred_element_type=jnp.float32
    )


def local(latent, cotangent, resample_weight, conv_weight, norm_gain):
    frames, low_rows, low_cols, in_chan = latent.shape
    height, width, channels = (2 * low_rows, 2 * low_cols, conv_weight.shape[-1])
    flat_two = resample_weight.reshape(9 * in_chan, channels)
    latent_border = with_halo(latent, (("rows", 1), ("cols", 2)), 1)
    lifted = upsample(latent_border)[:, 1:-1, 1:-1]
    own_taps = taps_plane(lifted, height, width)
    resampled = jnp.dot(
        own_taps.reshape(-1, 9 * in_chan), flat_two, preferred_element_type=jnp.float32
    ).astype(jnp.bfloat16)
    z_float = resampled.astype(jnp.float32).reshape(frames, height, width, channels)
    inverse, normed, scaled, sigma, hidden = statistics(z_float, norm_gain)
    hidden_border = with_halo(hidden, (("rows", 1), ("cols", 2)), 1)
    earlier = from_behind(hidden_border[-2:], "tm", 1)
    extended = jnp.concatenate([earlier, hidden_border], axis=0)
    grad_border = with_halo(cotangent, (("rows", 1), ("cols", 2)), 1)
    later = from_behind(grad_border[:2], "tm", -1)
    grad_ext = jnp.concatenate([grad_border, later], axis=0)
    flip_three = jnp.transpose(jnp.flip(conv_weight, (0, 1, 2)), (0, 1, 2, 4, 3)).reshape(
        27 * channels, channels
    )
    hidden_grad = jnp.dot(
        taps_volume(grad_ext, frames, height, width).reshape(-1, 27 * channels),
        flip_three,
        preferred_element_type=jnp.float32,
    ).reshape(frames, height, width, channels)
    scaled_grad = hidden_grad * sigma * (1.0 + scaled * (1.0 - sigma))
    gain_local = jnp.sum(scaled_grad * normed, axis=(0, 1, 2))
    normed_grad = scaled_grad * norm_gain
    delta = (
        inverse * (normed_grad - normed * jnp.mean(normed_grad * normed, axis=-1, keepdims=True))
    ).astype(jnp.bfloat16)
    grad_flat = cotangent.reshape(-1, channels)
    conv_local = contract_rows(
        taps_volume(extended, frames, height, width).reshape(-1, 27 * channels), grad_flat
    ).reshape(-1)
    delta_border = with_halo(delta, (("rows", 1), ("cols", 2)), 1)
    flip_two = jnp.transpose(jnp.flip(resample_weight, (0, 1)), (0, 1, 3, 2)).reshape(
        9 * channels, in_chan
    )
    lifted_grad = jnp.dot(
        taps_plane(delta_border, height, width).reshape(-1, 9 * channels),
        flip_two,
        preferred_element_type=jnp.float32,
    )
    grad_input = (
        lifted_grad.reshape(frames, low_rows, 2, low_cols, 2, in_chan)
        .sum(axis=(2, 4))
        .astype(jnp.bfloat16)
    )
    resample_local = contract_rows(
        own_taps.reshape(-1, 9 * in_chan), delta.reshape(-1, channels)
    ).reshape(-1)
    devices_all = lax.axis_size(("tm", "rows", "cols"))
    share_two = resample_local.shape[0] // devices_all
    resample_total, grad_gain = lax.psum((resample_local, gain_local), ("tm", "rows", "cols"))
    my_index = lax.axis_index(("tm", "rows", "cols"))
    grad_resample = lax.dynamic_slice_in_dim(resample_total, my_index * share_two, share_two)
    grad_conv = lax.psum_scatter(
        conv_local, ("tm", "rows", "cols"), scatter_dimension=0, tiled=True
    )
    return (grad_input, grad_resample, grad_conv, grad_gain)


def solution(mesh):
    in_specs = (P("tm", "rows", "cols", None), P("tm", "rows", "cols", None), P(), P(), P())
    out_specs = (
        P("tm", "rows", "cols", None),
        P(("tm", "rows", "cols")),
        P(("tm", "rows", "cols")),
        P(),
    )
    return jax.shard_map(local, mesh=mesh, in_specs=in_specs, out_specs=out_specs, check_vma=False)
```

profile of v0, /device:TPU:57, one launch (start us, length us, event | category | flops | bytes accessed | tf_op | source)
XLA Modules:
  0.0 426.0 jit_solution(5408776880432605088)
XLA Ops:
  8.0 4.5 %collective-permute-start = (bf16[3,1,8,384]{3,2,1,0:T(8,128)(2,1)S(1)}, bf16[3,1,8,384]{3,2,1,0:T(8,128)(2,1)S(1)}, u32[]{:S(2)}, u32[]{:S(2)}) collective-permute-start(bf16[3,1,8,384]{3,2,1,0:T(8,128)(2,1)S(1)} %get-tuple-element.102), channel_id=1, source_target_pairs={{0,8},{8,16},{16,24},{24,32},{32,40},{40,48},{48,56},{1,9},{9,17},... | collective-permute-start | bytes 55304 | tf_op jit(solution)/shard_map/ppermute | solution.py:16
  12.5 1.9 collective-permute-start.1
  15.2 1.9 collective-permute-start.5
  17.1 3.8 collective-permute-start.4
  20.9 1.9 reverse_bitcast_fusion
  22.9 2.4 copy.36
  25.2 4.1 reshape.72
  29.4 3.6 copy.37
  33.7 1.3 collective-permute-start.7
  35.0 4.0 collective-permute-start.6
  39.1 1.3 collective-permute-start.3
  40.4 4.0 collective-permute-start.2
  44.5 3.0 collective-permute-start.8
  53.5 4.6 %concatenate.98 = bf16[3,4,16,5184]{3,2,1,0:T(8,128)(2,1)} concatenate(bf16[3,4,16,192]{3,2,1,0:T(8,128)(2,1)} %get-tuple-element.82, bf16[3,4,16,192]{3,2,1,0:T(8,128)(2,1)} %get-tuple-element.95, bf16[3,4,16,192]{3,2,1,0:T(8,128)(2,1)} %get-tuple-element.68, bf16[3,4,16,192]{3,2,1,0:T(8,128)(2,1)} %get-tuple-element.81, bf16[3,4,16,192]{3,2,1,0:T(8,128)(2,1)S(1)} %copy-done.4, ...), dimensions={3} | concatenate | bytes 3981312 | tf_op jit(solution)/shard_map/concatenate | solution.py:44
  58.1 2.5 multiply_reduce_fusion
  60.8 2.1 collective-permute-start.14
  62.9 3.9 collective-permute-start.13
  66.8 2.5 convolution_bitcast_fusion.1
  69.3 5.0 %reshape.76 = f32[663552]{0:T(1024)} reshape(f32[3456,192]{1,0:T(8,128)} %convolution_bitcast_fusion.1) | data formatting | bytes 5308416 | tf_op jit(solution)/shard_map/reshape | solution.py:121
  75.6 4.0 collective-permute-start.15
  82.8 5.4 %collective-permute-done.17 = bf16[2,6,18,192]{3,2,1,0:T(8,128)(2,1)S(1)} collective-permute-done((bf16[2,6,18,192]{3,2,1,0:T(8,128)(2,1)S(1)}, bf16[2,6,18,192]{3,2,1,0:T(8,128)(2,1)S(1)}, u32[]{:S(2)}, u32[]{:S(2)}) %collective-permute-start.17) | collective-permute-done | bytes 82976 | tf_op jit(solution)/shard_map/ppermute | solution.py:25
  89.3 4.4 %concatenate.112 = bf16[3,4,16,5184]{3,2,1,0:T(8,128)(2,1)S(1)} concatenate(bf16[3,4,16,192]{3,2,1,0:T(8,128)(2,1)} %get-tuple-element.25, bf16[3,4,16,192]{3,2,1,0:T(8,128)(2,1)} %get-tuple-element.24, bf16[3,4,16,192]{3,2,1,0:T(8,128)(2,1)} %get-tuple-element.23, bf16[3,4,16,192]{3,2,1,0:T(8,128)(2,1)} %get-tuple-element.22, bf16[3,4,16,192]{3,2,1,0:T(8,128)(2,1)} %get-tuple-element.21, ...), dimensions={3} | concatenate | bytes 3981312 | tf_op jit(solution)/shard_map/concatenate | solution.py:44
  93.8 3.3 convolution_bitcast_fusion
  97.0 6.6 %reshape.77 = f32[995328]{0:T(1024)} reshape(f32[5184,192]{1,0:T(8,128)} %convolution_bitcast_fusion) | data formatting | bytes 7962624 | tf_op jit(solution)/shard_map/reshape | solution.py:104
  103.7 2.5 collective-permute-start.10
  106.2 4.1 collective-permute-start.9
  110.5 119.3 %psum.15 = f32[192]{0:T(256)} all-reduce(f32[192]{0:T(256)S(1)} %get-tuple-element.4), channel_id=1, replica_groups=mesh['tm'=8,'rows'=8,'cols'=8] {'tm','rows','cols'}, use_global_device_ids=true, to_apply=%region_6.7 | all-reduce | flops 192 | bytes 1536 | tf_op jit(solution)/shard_map/psum | solution.py:124
  231.1 4.2 collective-permute-start.11
  237.1 1.6 convolution_reduce_fusion
  238.6 177.7 %all-reduce.4.cloned.1.call-done = (f32[663552]{0:T(1024)}, f32[995328]{0:T(1024)}) async-done(((f32[663552]{0:T(1024)}, f32[995328]{0:T(1024)}), (f32[663552]{0:T(1024)}, f32[995328]{0:T(1024)})) %all-reduce.4.cloned.1.call-update) | async-done | bytes 6635536 | tf_op jit(solution)/shard_map/psum | solution.py:124
  416.4 1.4 dynamic_slice.3
  417.8 1.4 dynamic-slice
  (92 shorter events, 17.3 us)
Async XLA Ops:
  7.2 409.2 %all-reduce.4.cloned.1.call-start = ((), (), s32[]{:S(2)}) async-start(), calls=%async_computation | async-start | bytes 13271040 | tf_op jit(solution)/shard_map/psum | solution.py:124
  8.0 25.7 %collective-permute-start = (bf16[3,1,8,384]{3,2,1,0:T(8,128)(2,1)S(1)}, bf16[3,1,8,384]{3,2,1,0:T(8,128)(2,1)S(1)}, u32[]{:S(2)}, u32[]{:S(2)}) collective-permute-start(bf16[3,1,8,384]{3,2,1,0:T(8,128)(2,1)S(1)} %get-tuple-element.102), channel_id=1, source_target_pairs={{0,8},{8,16},{16,24},{24,32},{32,40},{40,48},{48,56},{1,9},{9,17},... | collective-permute-start | bytes 55304 | tf_op jit(solution)/shard_map/ppermute | solution.py:16
  12.5 26.5 %collective-permute-start.1 = (bf16[3,1,8,384]{3,2,1,0:T(8,128)(2,1)S(1)}, bf16[3,1,8,384]{3,2,1,0:T(8,128)(2,1)S(1)}, u32[]{:S(2)}, u32[]{:S(2)}) collective-permute-start(bf16[3,1,8,384]{3,2,1,0:T(8,128)(2,1)S(1)} %get-tuple-element.101), channel_id=1, source_target_pairs={{8,0},{16,8},{24,16},{32,24},{40,32},{48,40},{56,48},{9,1},{17,9},... | collective-permute-start | bytes 55304 | tf_op jit(solution)/shard_map/ppermute | solution.py:17
  15.2 17.7 %collective-permute-start.5 = (bf16[3,1,16,192]{3,2,1,0:T(8,128)(2,1)S(1)}, bf16[3,1,16,192]{3,2,1,0:T(8,128)(2,1)S(1)}, u32[]{:S(2)}, u32[]{:S(2)}) collective-permute-start(bf16[3,1,16,192]{3,2,1,0:T(8,128)(2,1)S(1)} %get-tuple-element.97), channel_id=1, source_target_pairs={{8,0},{16,8},{24,16},{32,24},{40,32},{48,40},{56,48},{9,1},{17,9},... | collective-permute-start | bytes 55304 | tf_op jit(solution)/shard_map/ppermute | solution.py:17
  17.1 5.7 %copy-start = (bf16[3,3,384,192]{2,3,1,0:T(8,128)(2,1)S(1)}, bf16[3,3,384,192]{2,3,1,0:T(8,128)(2,1)}, u32[]{:S(2)}) copy-start(bf16[3,3,384,192]{2,3,1,0:T(8,128)(2,1)} %param.7) | copy-start | bytes 3981316
  17.1 15.8 %collective-permute-start.4 = (bf16[3,1,16,192]{3,2,1,0:T(8,128)(2,1)S(1)}, bf16[3,1,16,192]{3,2,1,0:T(8,128)(2,1)S(1)}, u32[]{:S(2)}, u32[]{:S(2)}) collective-permute-start(bf16[3,1,16,192]{3,2,1,0:T(8,128)(2,1)S(1)} %get-tuple-element.98), channel_id=1, source_target_pairs={{0,8},{8,16},{16,24},{24,32},{32,40},{40,48},{48,56},{1,9},{9,17},... | collective-permute-start | bytes 55304 | tf_op jit(solution)/shard_map/ppermute | solution.py:16
  29.3 3.6 copy-start.4
  29.4 4.4 %copy-start.6 = (bf16[3,2,8,384]{3,2,1,0:T(8,128)(2,1)S(1)}, bf16[3,2,8,384]{3,2,1,0:T(8,128)(2,1)}, u32[]{:S(2)}) copy-start(bf16[3,2,8,384]{3,2,1,0:T(8,128)(2,1)} %param.5) | copy-start | bytes 110596
  33.7 10.7 %collective-permute-start.7 = (bf16[3,6,1,192]{3,2,1,0:T(2,128)(2,1)S(1)}, bf16[3,6,1,192]{3,2,1,0:T(2,128)(2,1)S(1)}, u32[]{:S(2)}, u32[]{:S(2)}) collective-permute-start(bf16[3,6,1,192]{3,2,1,0:T(2,128)(2,1)S(1)} %get-tuple-element.84), channel_id=1, source_target_pairs={{1,0},{2,1},{3,2},{4,3},{5,4},{6,5},{7,6},{9,8},{10,9},{11,10},{12... | collective-permute-start | bytes 20744 | tf_op jit(solution)/shard_map/ppermute | solution.py:17
  35.0 9.4 %collective-permute-start.6 = (bf16[3,6,1,192]{3,2,1,0:T(2,128)(2,1)S(1)}, bf16[3,6,1,192]{3,2,1,0:T(2,128)(2,1)S(1)}, u32[]{:S(2)}, u32[]{:S(2)}) collective-permute-start(bf16[3,6,1,192]{3,2,1,0:T(2,128)(2,1)S(1)} %get-tuple-element.85), channel_id=1, source_target_pairs={{0,1},{1,2},{2,3},{3,4},{4,5},{5,6},{6,7},{8,9},{9,10},{10,11},{11... | collective-permute-start | bytes 20744 | tf_op jit(solution)/shard_map/ppermute | solution.py:16
  39.1 9.4 %collective-permute-start.3 = (bf16[3,4,1,384]{3,2,1,0:T(2,128)(2,1)S(1)}, bf16[3,4,1,384]{3,2,1,0:T(2,128)(2,1)S(1)}, u32[]{:S(2)}, u32[]{:S(2)}) collective-permute-start(bf16[3,4,1,384]{3,2,1,0:T(2,128)(2,1)S(1)} %get-tuple-element.100), channel_id=1, source_target_pairs={{1,0},{2,1},{3,2},{4,3},{5,4},{6,5},{7,6},{9,8},{10,9},{11,10},{12... | collective-permute-start | bytes 27656 | tf_op jit(solution)/shard_map/ppermute | solution.py:17
  40.4 8.1 %collective-permute-start.2 = (bf16[3,4,1,384]{3,2,1,0:T(2,128)(2,1)S(1)}, bf16[3,4,1,384]{3,2,1,0:T(2,128)(2,1)S(1)}, u32[]{:S(2)}, u32[]{:S(2)}) collective-permute-start(bf16[3,4,1,384]{3,2,1,0:T(2,128)(2,1)S(1)} %get-tuple-element.99), channel_id=1, source_target_pairs={{0,1},{1,2},{2,3},{3,4},{4,5},{5,6},{6,7},{8,9},{9,10},{10,11},{11... | collective-permute-start | bytes 27656 | tf_op jit(solution)/shard_map/ppermute | solution.py:16
  44.5 7.7 %collective-permute-start.8 = (bf16[2,6,18,192]{3,2,1,0:T(8,128)(2,1)S(1)}, bf16[2,6,18,192]{3,2,1,0:T(8,128)(2,1)S(1)}, u32[]{:S(2)}, u32[]{:S(2)}) collective-permute-start(bf16[2,6,18,192]{3,2,1,0:T(8,128)(2,1)S(1)} %pad_maximum_fusion.7), channel_id=1, source_target_pairs={{64,0},{128,64},{192,128},{256,192},{320,256},{384,320},{448,384},... | collective-permute-start | bytes 248840 | tf_op jit(solution)/shard_map/ppermute | solution.py:25
  49.4 1.5 copy-start.3
  49.7 2.4 copy-start.7
  53.4 4.6 %copy-start.2 = (bf16[3,3,3,192,192]{4,3,2,1,0:T(8,128)(2,1)S(1)}, bf16[3,3,3,192,192]{4,3,2,1,0:T(8,128)(2,1)}, u32[]{:S(2)}) copy-start(bf16[3,3,3,192,192]{4,3,2,1,0:T(8,128)(2,1)} %copy.37) | copy-start | bytes 5971972
  53.4 4.6 %copy-start.9 = (f32[192]{0:T(256)S(1)}, f32[192]{0:T(256)}, u32[]{:S(2)}) copy-start(f32[192]{0:T(256)} %param.9) | copy-start | bytes 2308
  58.0 2.5 copy-start.5
  58.1 8.7 %copy-start.8 = (bf16[3,4,16,3456]{3,2,1,0:T(8,128)(2,1)S(1)}, bf16[3,4,16,3456]{3,2,1,0:T(8,128)(2,1)}, u32[]{:S(2)}) copy-start(bf16[3,4,16,3456]{3,2,1,0:T(8,128)(2,1)} %copy-done.7) | copy-start | bytes 3981316
  60.8 13.5 %collective-permute-start.14 = (bf16[3,1,16,192]{3,2,1,0:T(8,128)(2,1)S(1)}, bf16[3,1,16,192]{3,2,1,0:T(8,128)(2,1)S(1)}, u32[]{:S(2)}, u32[]{:S(2)}) collective-permute-start(bf16[3,1,16,192]{3,2,1,0:T(8,128)(2,1)S(1)} %get-tuple-element.89), channel_id=1, source_target_pairs={{8,0},{16,8},{24,16},{32,24},{40,32},{48,40},{56,48},{9,1},{17,9},... | collective-permute-start | bytes 55304 | tf_op jit(solution)/shard_map/ppermute | solution.py:17
  62.9 11.4 %collective-permute-start.13 = (bf16[3,1,16,192]{3,2,1,0:T(8,128)(2,1)S(1)}, bf16[3,1,16,192]{3,2,1,0:T(8,128)(2,1)S(1)}, u32[]{:S(2)}, u32[]{:S(2)}) collective-permute-start(bf16[3,1,16,192]{3,2,1,0:T(8,128)(2,1)S(1)} %get-tuple-element.88), channel_id=1, source_target_pairs={{0,8},{8,16},{16,24},{24,32},{32,40},{40,48},{48,56},{1,9},{9,17},... | collective-permute-start | bytes 55304 | tf_op jit(solution)/shard_map/ppermute | solution.py:16
  74.3 6.0 %collective-permute-start.16 = (bf16[3,6,1,192]{3,2,1,0:T(2,128)(2,1)S(1)}, bf16[3,6,1,192]{3,2,1,0:T(2,128)(2,1)S(1)}, u32[]{:S(2)}, u32[]{:S(2)}) collective-permute-start(bf16[3,6,1,192]{3,2,1,0:T(2,128)(2,1)S(1)} %get-tuple-element.76), channel_id=1, source_target_pairs={{1,0},{2,1},{3,2},{4,3},{5,4},{6,5},{7,6},{9,8},{10,9},{11,10},{12... | collective-permute-start | bytes 20744 | tf_op jit(solution)/shard_map/ppermute | solution.py:17
  75.6 4.9 %collective-permute-start.15 = (bf16[3,6,1,192]{3,2,1,0:T(2,128)(2,1)S(1)}, bf16[3,6,1,192]{3,2,1,0:T(2,128)(2,1)S(1)}, u32[]{:S(2)}, u32[]{:S(2)}) collective-permute-start(bf16[3,6,1,192]{3,2,1,0:T(2,128)(2,1)S(1)} %get-tuple-element.75), channel_id=1, source_target_pairs={{0,1},{1,2},{2,3},{3,4},{4,5},{5,6},{6,7},{8,9},{9,10},{10,11},{11... | collective-permute-start | bytes 20744 | tf_op jit(solution)/shard_map/ppermute | solution.py:16
  80.6 7.6 %collective-permute-start.17 = (bf16[2,6,18,192]{3,2,1,0:T(8,128)(2,1)S(1)}, bf16[2,6,18,192]{3,2,1,0:T(8,128)(2,1)S(1)}, u32[]{:S(2)}, u32[]{:S(2)}) collective-permute-start(bf16[2,6,18,192]{3,2,1,0:T(8,128)(2,1)S(1)} %pad_maximum_fusion.3), channel_id=1, source_target_pairs={{0,64},{64,128},{128,192},{192,256},{256,320},{320,384},{384,448},... | collective-permute-start | bytes 248840 | tf_op jit(solution)/shard_map/ppermute | solution.py:25
  103.6 6.7 %copy-start.1 = (bf16[3,3,384,192]{2,3,1,0:T(8,128)(2,1)S(1)}, bf16[3,3,384,192]{2,3,1,0:T(8,128)(2,1)}, u32[]{:S(2)}) copy-start(bf16[3,3,384,192]{2,3,1,0:T(8,128)(2,1)} %param.7) | copy-start | bytes 3981316
  103.7 126.1 %collective-permute-start.10 = (bf16[3,1,16,192]{3,2,1,0:T(8,128)(2,1)S(1)}, bf16[3,1,16,192]{3,2,1,0:T(8,128)(2,1)S(1)}, u32[]{:S(2)}, u32[]{:S(2)}) collective-permute-start(bf16[3,1,16,192]{3,2,1,0:T(8,128)(2,1)S(1)} %get-tuple-element.93), channel_id=1, source_target_pairs={{8,0},{16,8},{24,16},{32,24},{40,32},{48,40},{56,48},{9,1},{17,9},... | collective-permute-start | bytes 55304 | tf_op jit(solution)/shard_map/ppermute | solution.py:17
  106.2 123.5 %collective-permute-start.9 = (bf16[3,1,16,192]{3,2,1,0:T(8,128)(2,1)S(1)}, bf16[3,1,16,192]{3,2,1,0:T(8,128)(2,1)S(1)}, u32[]{:S(2)}, u32[]{:S(2)}) collective-permute-start(bf16[3,1,16,192]{3,2,1,0:T(8,128)(2,1)S(1)} %get-tuple-element.92), channel_id=1, source_target_pairs={{0,8},{8,16},{16,24},{24,32},{32,40},{40,48},{48,56},{1,9},{9,17},... | collective-permute-start | bytes 55304 | tf_op jit(solution)/shard_map/ppermute | solution.py:16
  229.8 5.6 %collective-permute-start.12 = (bf16[3,6,1,192]{3,2,1,0:T(2,128)(2,1)S(1)}, bf16[3,6,1,192]{3,2,1,0:T(2,128)(2,1)S(1)}, u32[]{:S(2)}, u32[]{:S(2)}) collective-permute-start(bf16[3,6,1,192]{3,2,1,0:T(2,128)(2,1)S(1)} %get-tuple-element.79), channel_id=1, source_target_pairs={{1,0},{2,1},{3,2},{4,3},{5,4},{6,5},{7,6},{9,8},{10,9},{11,10},{12... | collective-permute-start | bytes 20744 | tf_op jit(solution)/shard_map/ppermute | solution.py:17
  231.1 5.1 %collective-permute-start.11 = (bf16[3,6,1,192]{3,2,1,0:T(2,128)(2,1)S(1)}, bf16[3,6,1,192]{3,2,1,0:T(2,128)(2,1)S(1)}, u32[]{:S(2)}, u32[]{:S(2)}) collective-permute-start(bf16[3,6,1,192]{3,2,1,0:T(2,128)(2,1)S(1)} %get-tuple-element.80), channel_id=1, source_target_pairs={{0,1},{1,2},{2,3},{3,4},{4,5},{5,6},{6,7},{8,9},{9,10},{10,11},{11... | collective-permute-start | bytes 20744 | tf_op jit(solution)/shard_map/ppermute | solution.py:16
Sparse Core Ops, SparseCore 0:
  103.8 312.5 all-reduce.3
where the time goes:
time: 431 us; the launch traced here: 426 us
  waiting for transfers between devices  184 us (43%)
  blocking collectives  119 us (28%)
  starting transfers between devices  50.4 us (12%)
  local copies, waits for them, and re-layouts  43 us (10%)
  between operations  14.6 us (3%)
  matrix products  11 us (3%)
    psum x1, waiting for transfers between devices, local(): lax.psum((resample_local, gain_local), ('tm', 'rows', 'cols'))  178 us
    psum x1, blocking collectives, local(): lax.psum((resample_local, gain_local), ('tm', 'rows', 'cols'))  119 us
    ppermute x8, starting transfers between devices, with_halo(): before = lax.ppermute(last, axis, up)  32.5 us
    ppermute x8, starting transfers between devices, with_halo(): after = lax.ppermute(first, axis, down)  13.6 us
    concatenate x2, local copies, waits for them, and re-layouts, taps_volume(): jnp.concatenate([source[step_t:step_t + frames, step_y:step_y + height, s...  8.97 us
  transfers between devices with their start and end apart: 19, of which 4 were waited for; matrix products, arithmetic and copies ran while one was open for 7% of the time, Pallas kernels for 0%

commit v1 on v0

v1 whole, which is shorter than its diff:
```python
import functools

import jax
import jax.numpy as jnp
import numpy as np
from jax import lax
from jax.experimental import pallas as pl
from jax.experimental.pallas import tpu as pltpu
from jax.sharding import PartitionSpec as P

EPSILON = 1e-06
MESH = pl.DeviceIdType.MESH
BF = jnp.bfloat16
F32 = jnp.float32


def selectors():
    low = [0, 1, 1, 2, 2, 3]

    def zeros(*dims):
        return np.zeros(dims, np.float32)

    widen = zeros(96, 48)
    for t in range(3):
        for l in range(2):
            for c in range(16):
                widen[t * 32 + l * 16 + c, t * 16 + l * 8 + c // 2] = 1
    even_192, even_384 = zeros(192, 192), zeros(384, 384)
    for u in range(96):
        even_192[2 * u, u] = even_192[2 * u + 1, 96 + u] = 1
    for u in range(192):
        even_384[2 * u, u] = even_384[2 * u + 1, 192 + u] = 1
    lift, lift_rim = zeros(3, 96, 64), zeros(2, 3, 96, 16)
    cot, cot_rim = zeros(2, 96, 96), zeros(2, 5, 96, 32)
    pair, pair_rim = zeros(3, 96, 96), zeros(2, 3, 96, 32)
    for row in range(6):
        for c in range(16):
            out = row * 16 + c
            par = row * 16 + (c % 2) * 8 + c // 2
            for j in range(3):
                at = c + j - 1
                if 0 <= at < 16:
                    lift[j, out, low[row] * 16 + at] = 1
                    pair[j, par, row * 16 + at] = 1
                    if j != 1:
                        cot[j // 2, out, row * 16 + at] = 1
                else:
                    side = j // 2
                    for f in range(5):
                        cot_rim[side, f, out, f * 6 + row] = 1
                    for f in range(3):
                        lift_rim[side, f, out, f * 4 + low[row]] = 1
                        pair_rim[side, f, par, f * 6 + row] = 1
    edge_cot, edge_low = zeros(64, 480), zeros(32, 192)
    for side, col in ((0, 0), (1, 15)):
        for n in range(30):
            edge_cot[side * 32 + n, n * 16 + col] = 1
        for n in range(12):
            edge_low[side * 16 + n, n * 16 + col] = 1
    parts = (widen, even_192, even_384, lift, lift_rim, cot, cot_rim, pair, pair_rim, edge_cot, edge_low)
    return [jnp.asarray(p, BF) for p in parts]


def mm(a, b):
    return jnp.dot(a, b, preferred_element_type=F32)


def mm_nt(a, b):
    return lax.dot_general(a, b, (((1,), (1,)), ((), ())), preferred_element_type=F32)


def mm_tn(a, b):
    return lax.dot_general(a, b, (((0,), (0,)), ((), ())), preferred_element_type=F32)


def kernel(
    latent_ref, cot_ref, gain_ref, wr_hbm, wc_hbm,
    widen, even_192, even_384, lift, lift_rim, cot, cot_rim, pair, pair_rim, edge_cot, edge_low,
    gi_ref, oc_ref, or_ref, og_ref,
    wr, wc, sc, lc, lcp, hs_c, hs_l, hs_d, rim_c, rim_l, rim_d, sl, slp, xd, sd,
    fc, fr, bs_c, br_c, xs_c, xr_c, ac_c, ys_c, yr_c,
    bs_r, br_r, xs_r, xr_r, ac_r, ys_r, yr_r,
    g_core, g_x, g_y, pw_c, pw_r, ws, land, flat_c, flat_r,
    load_sem, ssem, rsem, core_s, core_r, x_s, x_r, y_s, y_r, fin_s, fin_r,
    gc_s, gc_r, gx_s, gx_r, gy_s, gy_r,
):
    y, r, c = lax.axis_index("tm"), lax.axis_index("rows"), lax.axis_index("cols")
    h, zl = r % 2, r // 2
    x, zh = c % 4, c // 4
    z = zh * 4 + zl

    def dev(dy=0, dr=0, dc=0):
        return ((y + dy + 8) % 8, (r + dr + 8) % 8, (c + dc + 8) % 8)

    partner = (y, zl * 2 + 1 - h, c)

    def peer_x(o):
        return (y, r, zh * 4 + (x + o) % 4)

    load_r = pltpu.make_async_copy(wr_hbm, wr, load_sem.at[0])
    load_c = pltpu.make_async_copy(wc_hbm, wc, load_sem.at[1])
    load_r.start()
    load_c.start()

    bar = pltpu.get_barrier_semaphore()
    sources = [dev(0, 1), dev(0, -1), dev(1, 0), dev(1, 1), dev(1, -1), dev(0, 0, 1), dev(0, 0, -1), partner]
    sources += [peer_x(o) for o in range(1, 4)] + [dev(o) for o in range(1, 8)]
    for d in sources:
        pl.semaphore_signal(bar, inc=1, device_id=d, device_id_type=MESH)
    for q in range(8):
        src = (y, 2 * (q % 4) + r // 4, (q // 4) * 4 + r % 4)

        @pl.when(jnp.logical_or(src[1] != r, src[2] != c))
        def _():
            pl.semaphore_signal(bar, inc=1, device_id=src, device_id_type=MESH)

    mine = jnp.where(r == 4 * h + x, 1, 0)

    sc[1, 0:3, 1:5] = cot_ref[...]
    own_low = latent_ref[...].astype(F32).reshape(48, 384).astype(BF)
    lc[:, 1:3] = mm(widen[...], own_low).astype(BF).reshape(3, 2, 16, 384)

    pl.semaphore_wait(bar, len(sources) + 8 - mine)

    def remote(src, dst, n, to):
        return pltpu.make_async_remote_copy(
            src_ref=src, dst_ref=dst, send_sem=ssem.at[n], recv_sem=rsem.at[n],
            device_id=to, device_id_type=MESH,
        )

    f3, f2, late = pl.ds(0, 3), pl.ds(0, 2), pl.ds(3, 2)
    first = [
        remote(sc.at[1, f3, 1], sc.at[1, f3, 5], 0, dev(0, -1)),
        remote(sc.at[1, f3, 4], sc.at[1, f3, 0], 1, dev(0, 1)),
        remote(lc.at[f3, 1], lc.at[f3, 3], 5, dev(0, -1)),
        remote(lc.at[f3, 2], lc.at[f3, 0], 6, dev(0, 1)),
        remote(sc.at[1, f2, pl.ds(1, 4)], sc.at[1, late, pl.ds(1, 4)], 2, dev(-1, 0)),
        remote(sc.at[1, f2, 1], sc.at[1, late, 5], 3, dev(-1, -1)),
        remote(sc.at[1, f2, 4], sc.at[1, late, 0], 4, dev(-1, 1)),
    ]
    for copy in first:
        copy.start()
    for copy in first:
        copy.wait()

    @pl.when(r == 0)
    def _():
        sc[1, :, 0] = jnp.zeros((5, 16, 192), BF)
        lc[:, 0] = jnp.zeros((3, 16, 384), BF)

    @pl.when(r == 7)
    def _():
        sc[1, :, 5] = jnp.zeros((5, 16, 192), BF)
        lc[:, 3] = jnp.zeros((3, 16, 384), BF)

    @pl.when(y == 7)
    def _():
        sc[1, 3:5] = jnp.zeros((2, 6, 16, 192), BF)

    low_all = lc[...].reshape(192, 384)
    hs_l[...] = mm(edge_low[...], low_all).astype(BF)
    hs_c[...] = mm(edge_cot[...], sc[1].reshape(480, 192)).astype(BF)
    second = [
        remote(hs_l.at[pl.ds(0, 16)], rim_l.at[1], 9, dev(0, 0, -1)),
        remote(hs_l.at[pl.ds(16, 16)], rim_l.at[0], 10, dev(0, 0, 1)),
        remote(hs_c.at[pl.ds(0, 32)], rim_c.at[1], 7, dev(0, 0, -1)),
        remote(hs_c.at[pl.ds(32, 32)], rim_c.at[0], 8, dev(0, 0, 1)),
    ]
    for copy in second:
        copy.start()
    lcp[...] = mm(low_all, even_384[...]).astype(BF).reshape(3, 4, 16, 384)
    load_r.wait()
    load_c.wait()
    for copy in second:
        copy.wait()

    @pl.when(c == 0)
    def _():
        rim_l[0] = jnp.zeros((16, 384), BF)
        rim_c[0] = jnp.zeros((32, 192), BF)

    @pl.when(c == 7)
    def _():
        rim_l[1] = jnp.zeros((16, 384), BF)
        rim_c[1] = jnp.zeros((32, 192), BF)

    rim_p = [mm(rim_l[s], even_384[...]).astype(BF) for s in range(2)]
    for t in range(3):
        here = lc[t].reshape(64, 384)
        here_p = lcp[t].reshape(64, 384)
        for j in range(3):
            wide, wide_p = mm(lift[j], here), mm(lift[j], here_p)
            if j != 1:
                wide += mm(lift_rim[j // 2, t], rim_l[j // 2])
                wide_p += mm(lift_rim[j // 2, t], rim_p[j // 2])
            sl[j, t] = wide.astype(BF).reshape(6, 16, 384)
            slp[j, t] = wide_p.astype(BF).reshape(6, 16, 384)

    def fwd(i, total):
        for j in range(3):
            total += mm(sl[j, :, pl.ds(i, 4)].reshape(192, 384), wr[i, j])
        return total

    z_float = lax.fori_loop(0, 3, fwd, jnp.zeros((192, 192), F32)).astype(BF).astype(F32)
    gain = gain_ref[...]
    inverse = lax.rsqrt(jnp.mean(z_float * z_float, axis=-1, keepdims=True) + EPSILON)
    normed = z_float * inverse
    scaled = normed * gain
    sigma = 1.0 / (1.0 + jnp.exp(-scaled))
    hidden = (scaled * sigma).astype(BF)
    hidden_p = mm(hidden, even_192[...]).astype(BF)

    for f in range(5):
        here = sc[1, f].reshape(96, 192)
        for s in range(2):
            moved = mm(cot[s], here) + mm(cot_rim[s, f], rim_c[s])
            sc[2 * s, f] = moved.astype(BF).reshape(6, 16, 192)

    def cot_view(a, i, j):
        return sc[2 - j, pl.ds(2 - a, 3), pl.ds(2 - i, 4)].reshape(192, 192)

    def planes(both, half, dst, at):
        dst[0, pl.ds(at, half)] = both[:half, :128]
        dst[1, pl.ds(at, half)] = jnp.concatenate([both[:half, 128:], both[half:, :64]], axis=1)
        dst[2, pl.ds(at, half)] = both[half:, 64:]

    def conv_taps(n, carry):
        a, i = n // 3, n % 3
        for j in range(3):
            at = pl.multiple_of((n * 3 + j) * 96, 96)
            planes(mm_tn(hidden_p, cot_view(a, i, j)), 96, fc, at)
        return carry

    lax.fori_loop(0, 9, conv_taps, 0)

    lane_row = lax.broadcasted_iota(jnp.int32, (8, 128), 0)

    def block_c(hh, i, t):
        at = (81 * (t * 8 + 4 * hh + i)) // 2
        spare = jnp.zeros((8, 128), F32)
        for q in range(3):
            spare = jnp.where(lane_row == q, fc[q, pl.ds(at + 40, 1)], spare)
        return jnp.concatenate([fc[q, pl.ds(at, 40)] for q in range(3)] + [spare], axis=0)

    def block_r(hh, i, t):
        at = 27 * (t * 8 + 4 * hh + i)
        return jnp.concatenate([fr[q, pl.ds(at, 32)] for q in range(3)], axis=0)

    parts = {
        0: (block_c, bs_c, br_c, xs_c, xr_c, ac_c, ys_c, yr_c),
        1: (block_r, bs_r, br_r, xs_r, xr_r, ac_r, ys_r, yr_r),
    }

    def core_copy(part, o):
        _, bs, br = parts[part][:3]
        i = (x + o) % 4
        return pltpu.make_async_remote_copy(
            src_ref=bs.at[i], dst_ref=br.at[i], send_sem=core_s.at[part * 4 + o],
            recv_sem=core_r.at[part * 4 + o], device_id=partner, device_id_type=MESH)

    def x_copy(part, o):
        xs, xr = parts[part][3:5]
        n = part * 3 + o - 1
        return pltpu.make_async_remote_copy(
            src_ref=xs.at[o - 1], dst_ref=xr.at[o - 1], send_sem=x_s.at[n],
            recv_sem=x_r.at[n], device_id=peer_x(o), device_id_type=MESH)

    def y_copy(part, o):
        ys, yr = parts[part][6:8]
        n = part * 7 + o - 1
        return pltpu.make_async_remote_copy(
            src_ref=ys.at[(y + o) % 8], dst_ref=yr.at[o - 1], send_sem=y_s.at[n],
            recv_sem=y_r.at[n], device_id=dev(o), device_id_type=MESH)

    def core_send(part):
        block, bs = parts[part][:2]
        for o in (1, 2, 3, 0):
            i = (x + o) % 4

            def fill(t, carry):
                bs[i, t] = block(1 - h, i, t).astype(BF)
                return carry

            lax.fori_loop(0, 8, fill, 0)
            core_copy(part, o).start()

    def x_send(part):
        block, _, br, xs, _, ac = parts[part][:6]
        for o in (1, 2, 3, 0):
            i = (x + o) % 4
            core_copy(part, o).wait()

            def fill(t, carry):
                total = block(h, i, t) + br[i, t].astype(F32)
                if o:
                    xs[o - 1, t] = total.astype(BF)
                else:
                    ac[t] = total
                return carry

            lax.fori_loop(0, 8, fill, 0)
            if o:
                x_copy(part, o).start()

    def y_send(part):
        xr, ac, ys = parts[part][4:7]
        for o in range(1, 4):
            x_copy(part, o).wait()

        def fill(t, carry):
            total = ac[t]
            for k in range(3):
                total += xr[k, t].astype(F32)
            ac[t] = total
            ys[t] = total.astype(BF)
            return carry

        lax.fori_loop(0, 8, fill, 0)
        for o in range(1, 8):
            y_copy(part, o).start()

    def y_sum(part):
        ac, _, yr = parts[part][5:8]
        for o in range(1, 8):
            y_copy(part, o).wait()
        total = ac[y]
        for k in range(7):
            total += yr[k].astype(F32)
        return total

    core_send(0)

    def back(n, total):
        a, i = n // 3, n % 3
        for j in range(3):
            total += mm_nt(cot_view(a, i, j), wc[a, i, j])
        return total

    hidden_grad = lax.fori_loop(0, 9, back, jnp.zeros((192, 192), F32))
    scaled_grad = hidden_grad * sigma * (1.0 + scaled * (1.0 - sigma))
    gain_local = jnp.sum(scaled_grad * normed, axis=0, keepdims=True)
    normed_grad = scaled_grad * gain
    delta = (
        inverse * (normed_grad - normed * jnp.mean(normed_grad * normed, axis=-1, keepdims=True))
    ).astype(BF)
    xd[:, 1:5] = delta.reshape(3, 4, 16, 192)
    rows_d = [
        remote(xd.at[f3, 1], xd.at[f3, 5], 11, dev(0, -1)),
        remote(xd.at[f3, 4], xd.at[f3, 0], 12, dev(0, 1)),
    ]
    for copy in rows_d:
        copy.start()

    tail = jnp.concatenate([gain_local[:, 128:], jnp.zeros((1, 64), F32)], axis=1)
    g_core[h] = jnp.where(lane_row == 0, gain_local[:, :128], jnp.where(lane_row == 1, tail, 0.0))

    def small(buf, at, ss, rs, n, to):
        return pltpu.make_async_remote_copy(
            src_ref=buf.at[at], dst_ref=buf.at[at], send_sem=ss.at[n], recv_sem=rs.at[n],
            device_id=to, device_id_type=MESH)

    g1 = small(g_core, h, gc_s, gc_r, 0, partner)
    g1.start()

    x_send(0)

    def lift_taps(n, carry):
        for j in range(3):
            at = pl.multiple_of((n * 3 + j) * 192, 192)
            view = slp[j, :, pl.ds(n, 4)].reshape(192, 384)
            planes(mm_tn(view, delta), 192, fr, at)
        return carry

    lax.fori_loop(0, 3, lift_taps, 0)
    core_send(1)

    for copy in rows_d:
        copy.wait()

    @pl.when(r == 0)
    def _():
        xd[:, 0] = jnp.zeros((3, 16, 192), BF)

    @pl.when(r == 7)
    def _():
        xd[:, 5] = jnp.zeros((3, 16, 192), BF)

    hs_d[...] = mm(edge_cot[:, :288], xd[...].reshape(288, 192)).astype(BF)
    cols_d = [
        remote(hs_d.at[pl.ds(0, 32)], rim_d.at[1], 13, dev(0, 0, -1)),
        remote(hs_d.at[pl.ds(32, 32)], rim_d.at[0], 14, dev(0, 0, 1)),
    ]
    for copy in cols_d:
        copy.start()

    g1.wait()
    g_x[x] = g_core[0] + g_core[1]
    g2 = [small(g_x, x, gx_s, gx_r, o - 1, peer_x(o)) for o in range(1, 4)]
    for copy in g2:
        copy.start()

    x_send(1)

    for copy in g2:
        copy.wait()
    g_y[y] = (g_x[0] + g_x[1]) + (g_x[2] + g_x[3])
    g3 = [small(g_y, y, gy_s, gy_r, o - 1, dev(o)) for o in range(1, 8)]
    for copy in g3:
        copy.start()

    y_send(0)

    for copy in cols_d:
        copy.wait()

    @pl.when(c == 0)
    def _():
        rim_d[0] = jnp.zeros((32, 192), BF)

    @pl.when(c == 7)
    def _():
        rim_d[1] = jnp.zeros((32, 192), BF)

    for t in range(3):
        here = xd[t].reshape(96, 192)
        for j in range(3):
            moved = mm(pair[j], here)
            if j != 1:
                moved += mm(pair_rim[j // 2, t], rim_d[j // 2])
            sd[j, t] = moved.astype(BF).reshape(6, 16, 192)

    def unlift(i, total):
        for j in range(3):
            total += mm_nt(sd[2 - j, :, pl.ds(2 - i, 4)].reshape(192, 192), wr[i, j])
        return total

    lifted_grad = lax.fori_loop(0, 3, unlift, jnp.zeros((192, 384), F32))
    gi_ref[...] = lifted_grad.reshape(3, 2, 4, 8, 384).sum(axis=2).astype(BF)

    y_send(1)

    for copy in g3:
        copy.wait()
    g_sum = g_y[0]
    for k in range(1, 8):
        g_sum += g_y[k]
    g_hi = g_sum.astype(BF).astype(F32)
    g_lo = g_sum - g_hi

    pw_c[...] = jnp.zeros((3, 48, 128), F32)
    sum_c = y_sum(0)
    for q in range(3):
        pw_c[q, 0:40] = sum_c[40 * q : 40 * q + 40]
        pw_c[q, 40:41] = sum_c[120 + q : 121 + q]
    pw_r[...] = y_sum(1).reshape(3, 32, 128)

    def fin_copy(q):
        to = (y, 4 * h + x, q)
        remote_one = pltpu.make_async_remote_copy(
            src_ref=ws.at[q], dst_ref=land.at[z], send_sem=fin_s.at[q], recv_sem=fin_r.at[z],
            device_id=to, device_id_type=MESH)
        own = jnp.logical_and(to[1] == r, q == c)
        return remote_one, own

    for q in range(8):
        low = (27 * q) // 8
        for k in range(3):
            right = pw_r[k, low : low + 8]
            if k < 2:
                extra = (g_hi, g_lo)[k]
                right = jnp.where(lane_row == 5, extra[0:1], jnp.where(lane_row == 6, extra[1:2], right))
            both = jnp.concatenate([pw_c[k, 5 * q : 5 * q + 8], right], axis=0)
            ws[q, 16 * k : 16 * k + 16] = both.astype(BF)
        remote_one, own = fin_copy(q)

        @pl.when(jnp.logical_not(own))
        def _():
            remote_one.start()

        @pl.when(own)
        def _():
            pltpu.make_async_copy(ws.at[q], land.at[z], fin_r.at[z]).start()

    for q in range(8):
        remote_one, own = fin_copy(q)

        @pl.when(jnp.logical_not(own))
        def _():
            remote_one.wait_send()

    total = jnp.zeros((48, 128), F32)
    for k in range(8):
        pltpu.make_async_copy(ws.at[0], land.at[k], fin_r.at[k]).wait()
        total += land[k].astype(F32)

    og_ref[...] = jnp.where(
        lane_row == 0, total[13:14] + total[29:30], jnp.where(lane_row == 1, total[14:15] + total[30:31], 0.0)
    )
    flat_c[...] = jnp.zeros((24, 128), F32)
    flat_r[...] = jnp.zeros((24, 128), F32)
    for k in range(3):
        for u in range(6):
            flat_c[3 * u + k : 3 * u + k + 1] = total[16 * k + u : 16 * k + u + 1]
        for u in range(5):
            flat_r[3 * u + k : 3 * u + k + 1] = total[16 * k + 8 + u : 16 * k + 9 + u]

    def cut(flat, off):
        lane = lax.broadcasted_iota(jnp.int32, (16, 128), 1)
        m, s = off // 128, off % 128
        turn = (128 - s) % 128
        one = pltpu.roll(flat[pl.ds(m, 16)], turn, 1)
        two = pltpu.roll(flat[pl.ds(m + 1, 16)], turn, 1)
        return jnp.where(lane < 128 - s, one, two)

    oc_ref[...] = cut(flat_c, 192 * (r % 2) + 24 * c)
    or_ref[...] = cut(flat_r, 1296 * c - 384 * ((27 * c) // 8))


def local(latent, cotangent, resample_weight, conv_weight, norm_gain):
    vm, hbm = pl.BlockSpec(memory_space=pltpu.VMEM), pl.BlockSpec(memory_space=pl.ANY)
    consts = selectors()
    dma, V = pltpu.SemaphoreType.DMA, pltpu.VMEM
    c, s = 128, 96

    def reduce_buffers(n):
        return [
            V((4, 8, n, 128), BF), V((4, 8, n, 128), BF), V((3, 8, n, 128), BF), V((3, 8, n, 128), BF),
            V((8, n, 128), F32), V((8, n, 128), BF), V((7, n, 128), BF),
        ]

    scratch = [
        V((3, 3, 384, 192), BF), V((3, 3, 3, 192, 192), BF),
        V((3, 5, 6, 16, 192), BF), V((3, 4, 16, 384), BF), V((3, 4, 16, 384), BF),
        V((64, 192), BF), V((32, 384), BF), V((64, 192), BF),
        V((2, 32, 192), BF), V((2, 16, 384), BF), V((2, 32, 192), BF),
        V((3, 3, 6, 16, 384), BF), V((3, 3, 6, 16, 384), BF),
        V((3, 6, 16, 192), BF), V((3, 3, 6, 16, 192), BF),
        V((3, 2592 + 48, 128), F32), V((3, 1728 + 32, 128), F32),
        *reduce_buffers(c), *reduce_buffers(s),
        V((2, 8, 128), F32), V((4, 8, 128), F32), V((8, 8, 128), F32),
        V((3, 48, 128), F32), V((3, 32, 128), F32),
        V((8, 48, 128), BF), V((8, 48, 128), BF), V((24, 128), F32), V((24, 128), F32),
        dma((2,)), dma((15,)), dma((15,)), dma((8,)), dma((8,)), dma((6,)), dma((6,)), dma((14,)), dma((14,)),
        dma((8,)), dma((8,)), dma((1,)), dma((1,)), dma((3,)), dma((3,)), dma((7,)), dma((7,)),
    ]
    gi, oc, orr, og = pl.pallas_call(
        kernel,
        out_shape=[
            jax.ShapeDtypeStruct((3, 2, 8, 384), BF),
            jax.ShapeDtypeStruct((16, 128), F32),
            jax.ShapeDtypeStruct((16, 128), F32),
            jax.ShapeDtypeStruct((8, 128), F32),
        ],
        in_specs=[vm, vm, vm, hbm, hbm] + [vm] * len(consts),
        out_specs=[vm] * 4,
        scratch_shapes=scratch,
        compiler_params=pltpu.CompilerParams(
            collective_id=0, has_side_effects=True, vmem_limit_bytes=56 * 2**20
        ),
        cost_estimate=pl.CostEstimate(flops=1_600_000_000, bytes_accessed=5_000_000, transcendentals=40_000),
    )(latent, cotangent, norm_gain.reshape(1, 192), resample_weight, conv_weight, *consts)
    return gi, orr.reshape(-1)[:1296], oc.reshape(-1)[:1944], og.reshape(-1)[:192]


def solution(mesh):
    in_specs = (P("tm", "rows", "cols", None), P("tm", "rows", "cols", None), P(), P(), P())
    out_specs = (
        P("tm", "rows", "cols", None),
        P(("tm", "rows", "cols")),
        P(("tm", "rows", "cols")),
        P(),
    )
    return jax.shard_map(local, mesh=mesh, in_specs=in_specs, out_specs=out_specs, check_vma=False)
```

time: 431 us -> 84 us (0.19)
  the two profiles are of different devices: /device:TPU:57 before, /device:TPU:6 now
where the time goes in v1:
time: 84 us; the launch traced here: 83.6 us
  Pallas kernels  74.1 us (88%)
  local copies, waits for them, and re-layouts  8.89 us (11%)
    pallas_call x1, Pallas kernels, local(): pl.pallas_call(kernel, out_shape=[jax.ShapeDtypeStruct((3, 2, 8, 384), BF...  74.1 us
    unnamed x4, local copies, waits for them, and re-layouts  7.64 us

profile of v1, /device:TPU:6, one launch (start us, length us, event | category | flops | bytes accessed | tf_op | source)
XLA Modules:
  0.0 83.6 jit_solution(2492677608408475220)
XLA Ops:
  0.6 3.7 %copy.20.wr_hbm = bf16[3,3,384,192]{3,2,1,0:T(8,128)(2,1)} copy(bf16[3,3,384,192]{2,3,1,0:T(8,128)(2,1)} %param.18) | data formatting | bytes 2654208 | tf_op args[2]
  4.3 74.1 %shard_map.183 = (bf16[3,2,8,384]{3,2,1,0:T(8,128)(2,1)}, f32[16,128]{1,0:T(8,128)}, f32[16,128]{1,0:T(8,128)}, f32[8,128]{1,0:T(8,128)}) custom-call(bf16[3,2,8,384]{3,2,1,0:T(8,128)(2,1)} %latent_ref.1, bf16[3,4,16,192]{3,2,1,0:T(8,128)(2,1)} %cot_ref.1, f32[1,192]{1,0:T(1,128)} %bitcast.9, bf16[3,3,384,192]{3,2,1,0:T(8,128)(2,1)} %copy.20.wr_hbm, ...), custom_call_target="tpu_custom_call" | custom-call | flops 1600000000 | bytes 5000000 | tf_op jit(solution)/shard_map/pallas_call | solution.py:546
  78.4 1.2 %slice.11 = f32[192]{0:T(256)} slice(f32[1024]{0:T(1024)} %bitcast.8), slice={[0:192]} | slice | bytes 1536 | tf_op jit(solution)/shard_map/slice | solution.py:562
  79.6 1.4 %copy.24 = bf16[3,2,8,384]{3,2,1,0:T(8,128)(2,1)} copy(bf16[3,2,8,384]{3,2,1,0:T(8,128)(2,1)} %get-tuple-element.16) | data formatting | bytes 73728
  81.0 1.3 %copy.25 = f32[1296]{0:T(1024)} copy(f32[1296]{0:T(1024)} %bitcast.7) | data formatting | bytes 10368
  82.3 1.3 %copy.26 = f32[1944]{0:T(1024)} copy(f32[1944]{0:T(1024)} %bitcast.6) | data formatting | bytes 15552

commit v2 on v1

v2 whole, which is shorter than its diff:
```python
import functools

import jax
import jax.numpy as jnp
import numpy as np
from jax import lax
from jax.experimental import pallas as pl
from jax.experimental.pallas import tpu as pltpu
from jax.sharding import PartitionSpec as P

EPSILON = 1e-06
MESH = pl.DeviceIdType.MESH
BF = jnp.bfloat16
F32 = jnp.float32


def selectors():
    low = [0, 1, 1, 2, 2, 3]

    def zeros(*dims):
        return np.zeros(dims, np.float32)

    widen = zeros(96, 48)
    for t in range(3):
        for l in range(2):
            for c in range(16):
                widen[t * 32 + l * 16 + c, t * 16 + l * 8 + c // 2] = 1
    even_192, even_384 = zeros(192, 192), zeros(384, 384)
    for u in range(96):
        even_192[u, 2 * u] = even_192[96 + u, 2 * u + 1] = 1
    for u in range(192):
        even_384[2 * u, u] = even_384[2 * u + 1, 192 + u] = 1
    lift, lift_rim = zeros(3, 96, 64), zeros(2, 3, 96, 48)
    cot, cot_rim = zeros(2, 96, 96), zeros(2, 5, 96, 96)
    pair, pair_rim = zeros(3, 96, 96), zeros(2, 3, 96, 32)

    def slot(at, last, frame, late):
        kind = 1 if at == 0 else 2 if at == last else 0
        row = frame if kind else frame * (last - 1) + at - 1
        return (kind + 3 * late) * 16 + row

    for row in range(6):
        for c in range(16):
            out = row * 16 + c
            par = row * 16 + (c % 2) * 8 + c // 2
            for j in range(3):
                at = c + j - 1
                if 0 <= at < 16:
                    lift[j, out, low[row] * 16 + at] = 1
                    pair[j, par, row * 16 + at] = 1
                    if j != 1:
                        cot[j // 2, out, row * 16 + at] = 1
                else:
                    side = j // 2
                    for f in range(5):
                        cot_rim[side, f, out, slot(row, 5, f % 3, f // 3)] = 1
                    for f in range(3):
                        lift_rim[side, f, out, slot(low[row], 3, f, 0)] = 1
                        pair_rim[side, f, par, f * 6 + row] = 1
    edge_cot, edge_low, edge_delta = zeros(96, 192), zeros(96, 96), zeros(64, 288)
    for side, col in ((0, 0), (1, 15)):
        for n in range(18):
            edge_delta[side * 32 + n, n * 16 + col] = 1
        for t in range(3):
            for rows, edge in ((4, edge_cot), (2, edge_low)):
                for row in range(rows):
                    edge[side * 48 + t * rows + row, (t * rows + row) * 16 + col] = 1
                edge[side * 48 + 16 + t, t * rows * 16 + col] = 1
                edge[side * 48 + 32 + t, (t * rows + rows - 1) * 16 + col] = 1
    parts = (widen, even_192, even_384, lift, lift_rim, cot, cot_rim, pair, pair_rim, edge_cot, edge_low, edge_delta)
    return [jnp.asarray(p, BF) for p in parts]


def mm(a, b):
    return jnp.dot(a, b, preferred_element_type=F32)


def mm_nt(a, b):
    return lax.dot_general(a, b, (((1,), (1,)), ((), ())), preferred_element_type=F32)


def mm_tn(a, b):
    return lax.dot_general(a, b, (((0,), (0,)), ((), ())), preferred_element_type=F32)


def kernel(*refs):
    (latent_hbm, cot_hbm, gain_hbm, wr_hbm, wc_hbm), refs = refs[:5], refs[5:]
    const_hbm, (gi_ref, oc_ref, or_ref, og_ref), refs = refs[:12], refs[12:16], refs[16:]
    consts, refs = refs[:12], refs[12:]
    (widen, even_192, even_384, lift, lift_rim, cot, cot_rim, pair, pair_rim, edge_cot, edge_low, edge_delta) = consts
    (
        latv, gain_v, wr, wc, sc, lc, lcp, hs, rim, hs_d, rim_d, sl, slp, xd, sd, fc, fr,
        g_core, g_x, g_y, sum_c, pw_c, pw_r, ws_c, ws_r, land_c, land_r, pack, flat_c, flat_r,
        load_sem, ssem, rsem, core_s, core_r, x_s, x_r, y_s, y_r, fin_s, fin_r,
        gc_s, gc_r, gx_s, gx_r, gy_s, gy_r,
    ), refs = refs[:47], refs[47:]
    bufs = [refs[5 * p : 5 * p + 5] for p in range(3)]
    yr_c, yr_r = refs[18:20]
    y_bufs = [(refs[15], yr_c), (refs[16], yr_c), (refs[17], yr_r)]

    y, r, c = lax.axis_index("tm"), lax.axis_index("rows"), lax.axis_index("cols")
    h, zl = r % 2, r // 2
    x, zh = c % 4, c // 4
    z = zh * 4 + zl

    def dev(dy=0, dr=0, dc=0):
        return ((y + dy + 8) % 8, (r + dr + 8) % 8, (c + dc + 8) % 8)

    partner = (y, zl * 2 + 1 - h, c)

    def peer_x(o):
        return (y, r, zh * 4 + (x + o) % 4)

    bar = pltpu.get_barrier_semaphore()
    sources = [dev(dy, dr, dc) for dc in (1, -1, 0) for dr in (-1, 0, 1) for dy in (0, 1) if (dy, dr, dc) != (0, 0, 0)]
    sources += [partner] + [peer_x(o) for o in range(1, 4)] + [dev(o) for o in range(1, 8)]
    for d in sources:
        pl.semaphore_signal(bar, inc=1, device_id=d, device_id_type=MESH)
    for q in range(8):
        src = (y, 2 * (q % 4) + r // 4, (q // 4) * 4 + r % 4)

        @pl.when(jnp.logical_or(src[1] != r, src[2] != c))
        def _():
            pl.semaphore_signal(bar, inc=1, device_id=src, device_id_type=MESH)

    mine = jnp.where(r == 4 * h + x, 1, 0)

    f3, f2, late = pl.ds(0, 3), pl.ds(0, 2), pl.ds(3, 2)
    targets = [(latent_hbm, latv), (cot_hbm, sc.at[1, f3, pl.ds(1, 4)]), (gain_hbm, gain_v)]
    targets += [(a, b) for a, b in zip(const_hbm, consts)] + [(wr_hbm, wr), (wc_hbm, wc)]
    loads = [pltpu.make_async_copy(a, b, load_sem.at[n]) for n, (a, b) in enumerate(targets)]
    for copy in loads:
        copy.start()
    for copy in loads[:-2]:
        copy.wait()

    own_low = latv[...].astype(F32).reshape(48, 384).astype(BF)
    own_low = mm(widen[...], own_low).astype(BF)
    lc[:, 1:3] = own_low.reshape(3, 2, 16, 384)
    hs[:, :, :, 0:384] = mm(edge_low[...], own_low).astype(BF).reshape(2, 3, 16, 384)
    own_cot = sc[1, 0:3, 1:5].reshape(192, 192)
    hs[:, :, :, 384:576] = mm(edge_cot[...], own_cot).astype(BF).reshape(2, 3, 16, 192)

    pl.semaphore_wait(bar, len(sources) + 8 - mine)

    def remote(src, dst, n, to):
        return pltpu.make_async_remote_copy(
            src_ref=src, dst_ref=dst, send_sem=ssem.at[n], recv_sem=rsem.at[n],
            device_id=to, device_id_type=MESH,
        )

    halo = []
    for s, dc in ((0, -1), (1, 1)):
        for n, (tile, dy, dr) in enumerate(((0, 0, 0), (2, 0, 1), (1, 0, -1), (0, -1, 0), (2, -1, 1), (1, -1, -1))):
            halo.append(remote(hs.at[s, tile], rim.at[1 - s, n], 11 + 6 * s + n, dev(dy, dr, dc)))
    halo += [
        remote(lc.at[f3, 1], lc.at[f3, 3], 5, dev(0, -1)),
        remote(lc.at[f3, 2], lc.at[f3, 0], 6, dev(0, 1)),
        remote(sc.at[1, f3, 1], sc.at[1, f3, 5], 0, dev(0, -1)),
        remote(sc.at[1, f3, 4], sc.at[1, f3, 0], 1, dev(0, 1)),
        remote(sc.at[1, f2, pl.ds(1, 4)], sc.at[1, late, pl.ds(1, 4)], 2, dev(-1, 0)),
        remote(sc.at[1, f2, 1], sc.at[1, late, 5], 3, dev(-1, -1)),
        remote(sc.at[1, f2, 4], sc.at[1, late, 0], 4, dev(-1, 1)),
    ]
    for copy in halo:
        copy.start()
    for copy in loads[-2:]:
        copy.wait()
    for copy in halo:
        copy.wait()

    @pl.when(r == 0)
    def _():
        sc[1, :, 0] = jnp.zeros((5, 16, 192), BF)
        lc[:, 0] = jnp.zeros((3, 16, 384), BF)
        for n in (1, 4):
            rim[:, n] = jnp.zeros((2, 16, 576), BF)

    @pl.when(r == 7)
    def _():
        sc[1, :, 5] = jnp.zeros((5, 16, 192), BF)
        lc[:, 3] = jnp.zeros((3, 16, 384), BF)
        for n in (2, 5):
            rim[:, n] = jnp.zeros((2, 16, 576), BF)

    @pl.when(y == 7)
    def _():
        sc[1, 3:5] = jnp.zeros((2, 6, 16, 192), BF)
        rim[:, 3:6] = jnp.zeros((2, 3, 16, 576), BF)

    @pl.when(c == 0)
    def _():
        rim[0] = jnp.zeros((6, 16, 576), BF)

    @pl.when(c == 7)
    def _():
        rim[1] = jnp.zeros((6, 16, 576), BF)

    lcp[...] = mm(lc[...].reshape(192, 384), even_384[...]).astype(BF).reshape(3, 4, 16, 384)
    rim_l = [rim[s, 0:3, :, 0:384].reshape(48, 384) for s in range(2)]
    rim_p = [mm(rim_l[s], even_384[...]).astype(BF) for s in range(2)]
    for t in range(3):
        here = lc[t].reshape(64, 384)
        here_p = lcp[t].reshape(64, 384)
        for j in range(3):
            wide, wide_p = mm(lift[j], here), mm(lift[j], here_p)
            if j != 1:
                wide += mm(lift_rim[j // 2, t], rim_l[j // 2])
                wide_p += mm(lift_rim[j // 2, t], rim_p[j // 2])
            sl[j, t] = wide.astype(BF).reshape(6, 16, 384)
            slp[j, t] = wide_p.astype(BF).reshape(6, 16, 384)

    def fwd(i, total):
        for j in range(3):
            total += mm_nt(sl[j, :, pl.ds(i, 4)].reshape(192, 384), wr[i, j])
        return total

    z_float = lax.fori_loop(0, 3, fwd, jnp.zeros((192, 192), F32)).astype(BF).astype(F32)
    gain = gain_v[...]
    inverse = lax.rsqrt(jnp.mean(z_float * z_float, axis=-1, keepdims=True) + EPSILON)
    normed = z_float * inverse
    scaled = normed * gain
    sigma = 1.0 / (1.0 + jnp.exp(-scaled))
    hidden = (scaled * sigma).astype(BF)
    hidden_t = mm_nt(even_192[...], hidden).astype(BF)

    for f in range(5):
        here = sc[1, f].reshape(96, 192)
        for s in range(2):
            moved = mm(cot[s], here) + mm(cot_rim[s, f], rim[s, :, :, 384:576].reshape(96, 192))
            sc[2 * s, f] = moved.astype(BF).reshape(6, 16, 192)

    def cot_view(a, i, j):
        return sc[2 - j, pl.ds(2 - a, 3), pl.ds(2 - i, 4)].reshape(192, 192)

    def planes(both, half, dst, at):
        dst[0, pl.ds(at, half)] = both[:half, :128]
        dst[1, pl.ds(at, half)] = jnp.concatenate([both[:half, 128:], both[half:, :64]], axis=1)
        dst[2, pl.ds(at, half)] = both[half:, 64:]

    def conv_taps(n, carry):
        a, i = n // 3, n % 3
        for j in range(3):
            at = pl.multiple_of((n * 3 + j) * 96, 96)
            planes(mm(hidden_t, cot_view(a, i, j)), 96, fc, at)
        return carry

    lane_row = lax.broadcasted_iota(jnp.int32, (8, 128), 0)

    def block_c(hh, i, t):
        at = (81 * (t * 8 + 4 * hh + i)) // 2
        spare = jnp.zeros((8, 128), F32)
        for q in range(3):
            spare = jnp.where(lane_row == q, fc[q, pl.ds(at + 40, 1)], spare)
        return jnp.concatenate([fc[q, pl.ds(at, 40)] for q in range(3)] + [spare], axis=0)

    def block_r(hh, i, t):
        at = 27 * (t * 8 + 4 * hh + i)
        return jnp.concatenate([fr[q, pl.ds(at, 32)] for q in range(3)], axis=0)

    parts = [(block_c, 0, 4), (block_c, 4, 8), (block_r, 0, 8)]

    def core_copy(p, o):
        bs, br = bufs[p][:2]
        i = (x + o) % 4
        return pltpu.make_async_remote_copy(
            src_ref=bs.at[i], dst_ref=br.at[i], send_sem=core_s.at[p * 4 + o],
            recv_sem=core_r.at[p * 4 + o], device_id=partner, device_id_type=MESH)

    def x_copy(p, m):
        xs, xr = bufs[p][2:4]
        return pltpu.make_async_remote_copy(
            src_ref=xs.at[m], dst_ref=xr.at[m], send_sem=x_s.at[p * 6 + m],
            recv_sem=x_r.at[p * 6 + m], device_id=peer_x(1 if m % 2 == 0 else 3), device_id_type=MESH)

    def core_send(p):
        block, lo, hi = parts[p]
        bs = bufs[p][0]
        for o in (2, 1, 3, 0):
            i = (x + o) % 4

            def fill(t, carry):
                bs[i, t - lo] = block(1 - h, i, t).astype(BF)
                return carry

            lax.fori_loop(lo, hi, fill, 0)
            core_copy(p, o).start()

    def x_fill(p, m, i, first, last, relayed):
        block, lo, _ = parts[p]
        _, br, xs, xr = bufs[p][:4]

        def fill(t, carry):
            total = block(h, i, t) + br[i, t - lo].astype(F32)
            if relayed:
                total += xr[m - 4, t - first].astype(F32)
            xs[m, t - first] = total.astype(BF)
            return carry

        lax.fori_loop(first, last, fill, 0)
        x_copy(p, m).start()

    def x_first(p):
        block, lo, hi = parts[p]
        mid = (lo + hi) // 2
        br, ac = bufs[p][1], bufs[p][4]
        core_copy(p, 2).wait()
        x_fill(p, 0, (x + 2) % 4, lo, mid, False)
        x_fill(p, 1, (x + 2) % 4, mid, hi, False)
        core_copy(p, 1).wait()
        x_fill(p, 2, (x + 1) % 4, mid, hi, False)
        core_copy(p, 3).wait()
        x_fill(p, 3, (x + 3) % 4, lo, mid, False)
        core_copy(p, 0).wait()

        def keep(t, carry):
            ac[t - lo] = block(h, x, t) + br[x, t - lo].astype(F32)
            return carry

        lax.fori_loop(lo, hi, keep, 0)

    def x_second(p):
        _, lo, hi = parts[p]
        mid = (lo + hi) // 2
        x_copy(p, 0).wait()
        x_fill(p, 4, (x + 1) % 4, lo, mid, True)
        x_copy(p, 1).wait()
        x_fill(p, 5, (x + 3) % 4, mid, hi, True)

    def y_copy(p, t):
        ys, yr = y_bufs[p]
        n = (0, 4, 8)[p] + t - parts[p][1]
        return pltpu.make_async_remote_copy(
            src_ref=ys.at[t - parts[p][1]], dst_ref=yr.at[y], send_sem=y_s.at[n],
            recv_sem=y_r.at[min(p, 2) // 2 * 8 + y], device_id=(t, r, c), device_id_type=MESH)

    def y_send(p):
        _, lo, hi = parts[p]
        mid = (lo + hi) // 2
        xr, ac = bufs[p][3], bufs[p][4]
        ys = y_bufs[p][0]
        for m in range(2, 6):
            x_copy(p, m).wait()
        for first, last, one, two in ((lo, mid, 4, 3), (mid, hi, 5, 2)):

            def fill(t, carry):
                total = ac[t - lo] + xr[one, t - first].astype(F32) + xr[two, t - first].astype(F32)
                ac[t - lo] = total
                ys[t - lo] = total.astype(BF)
                return carry

            lax.fori_loop(first, last, fill, 0)
        for t in range(lo, hi):

            @pl.when(y != t)
            def _():
                y_copy(p, t).start()

    def y_wait_send(p):
        _, lo, hi = parts[p]
        for t in range(lo, hi):

            @pl.when(y != t)
            def _():
                y_copy(p, t).wait_send()

    def y_sum(p):
        _, lo, _ = parts[p]
        ac, yr = bufs[p][4], y_bufs[p][1]
        total = ac[y - lo]
        for o in range(1, 8):
            k = (y + o) % 8
            pltpu.make_async_copy(yr.at[k], yr.at[k], y_r.at[min(p, 2) // 2 * 8 + k]).wait()
            total += yr[k].astype(F32)
        return total

    lax.fori_loop(0, 5, conv_taps, 0)
    core_send(0)
    lax.fori_loop(5, 7, conv_taps, 0)
    x_first(0)
    lax.fori_loop(7, 9, conv_taps, 0)
    core_send(1)

    def back(n, total):
        a, i = n // 3, n % 3
        for j in range(3):
            total += mm_nt(cot_view(a, i, j), wc[a, i, j])
        return total

    hidden_grad = lax.fori_loop(0, 9, back, jnp.zeros((192, 192), F32))
    x_first(1)
    x_second(0)
    scaled_grad = hidden_grad * sigma * (1.0 + scaled * (1.0 - sigma))
    gain_local = jnp.sum(scaled_grad * normed, axis=0, keepdims=True)
    normed_grad = scaled_grad * gain
    delta = (
        inverse * (normed_grad - normed * jnp.mean(normed_grad * normed, axis=-1, keepdims=True))
    ).astype(BF)
    xd[:, 1:5] = delta.reshape(3, 4, 16, 192)
    rows_d = [
        remote(xd.at[f3, 1], xd.at[f3, 5], 7, dev(0, -1)),
        remote(xd.at[f3, 4], xd.at[f3, 0], 8, dev(0, 1)),
    ]
    for copy in rows_d:
        copy.start()

    tail = jnp.concatenate([gain_local[:, 128:], jnp.zeros((1, 64), F32)], axis=1)
    g_core[h] = jnp.where(lane_row == 0, gain_local[:, :128], jnp.where(lane_row == 1, tail, 0.0))

    def small(buf, at, ss, rs, n, to):
        return pltpu.make_async_remote_copy(
            src_ref=buf.at[at], dst_ref=buf.at[at], send_sem=ss.at[n], recv_sem=rs.at[n],
            device_id=to, device_id_type=MESH)

    g1 = small(g_core, h, gc_s, gc_r, 0, partner)
    g1.start()


    def lift_taps(n, carry):
        for j in range(3):
            at = pl.multiple_of((n * 3 + j) * 192, 192)
            view = slp[j, :, pl.ds(n, 4)].reshape(192, 384)
            planes(mm_tn(view, delta), 192, fr, at)
        return carry

    lax.fori_loop(0, 3, lift_taps, 0)
    core_send(2)
    x_second(1)
    x_first(2)

    for copy in rows_d:
        copy.wait()

    @pl.when(r == 0)
    def _():
        xd[:, 0] = jnp.zeros((3, 16, 192), BF)

    @pl.when(r == 7)
    def _():
        xd[:, 5] = jnp.zeros((3, 16, 192), BF)

    hs_d[...] = mm(edge_delta[...], xd[...].reshape(288, 192)).astype(BF)
    cols_d = [
        remote(hs_d.at[pl.ds(0, 32)], rim_d.at[1], 9, dev(0, 0, -1)),
        remote(hs_d.at[pl.ds(32, 32)], rim_d.at[0], 10, dev(0, 0, 1)),
    ]
    for copy in cols_d:
        copy.start()

    g1.wait()
    g_x[x] = g_core[0] + g_core[1]
    g2 = [small(g_x, x, gx_s, gx_r, o - 1, peer_x(o)) for o in range(1, 4)]
    for copy in g2:
        copy.start()

    y_send(0)
    x_second(2)

    for copy in g2:
        copy.wait()
    g_y[y] = (g_x[0] + g_x[1]) + (g_x[2] + g_x[3])
    g3 = [small(g_y, y, gy_s, gy_r, o - 1, dev(o)) for o in range(1, 8)]
    for copy in g3:
        copy.start()

    y_send(1)

    for copy in cols_d:
        copy.wait()

    @pl.when(c == 0)
    def _():
        rim_d[0] = jnp.zeros((32, 192), BF)

    @pl.when(c == 7)
    def _():
        rim_d[1] = jnp.zeros((32, 192), BF)

    for t in range(3):
        here = xd[t].reshape(96, 192)
        for j in range(3):
            moved = mm(pair[j], here)
            if j != 1:
                moved += mm(pair_rim[j // 2, t], rim_d[j // 2])
            sd[j, t] = moved.astype(BF).reshape(6, 16, 192)

    def unlift(i, total):
        for j in range(3):
            total += mm(sd[2 - j, :, pl.ds(2 - i, 4)].reshape(192, 192), wr[i, j])
        return total

    lifted_grad = lax.fori_loop(0, 3, unlift, jnp.zeros((192, 384), F32))
    gi_ref[...] = lifted_grad.reshape(3, 2, 4, 8, 384).sum(axis=2).astype(BF)

    y_send(2)

    for copy in g3:
        copy.wait()
    g_sum = g_y[0]
    for k in range(1, 8):
        g_sum += g_y[k]
    g_hi = g_sum.astype(BF).astype(F32)
    g_lo = g_sum - g_hi

    extra = jnp.concatenate([g_hi[0:2], g_lo[0:2], jnp.zeros((4, 128), F32)], axis=0)

    def fin_copy(n, q):
        to = (y, 4 * h + x, q)
        src, dst = ((ws_c, land_c), (ws_r, land_r))[n]
        remote_one = pltpu.make_async_remote_copy(
            src_ref=src.at[q], dst_ref=dst.at[z], send_sem=fin_s.at[n * 8 + q], recv_sem=fin_r.at[n * 8 + z],
            device_id=to, device_id_type=MESH)
        return remote_one, jnp.logical_and(to[1] == r, q == c)

    def fin_start(n, q):
        remote_one, own = fin_copy(n, q)
        src, dst = ((ws_c, land_c), (ws_r, land_r))[n]

        @pl.when(jnp.logical_not(own))
        def _():
            remote_one.start()

        @pl.when(own)
        def _():
            pltpu.make_async_copy(src.at[q], dst.at[z], fin_r.at[n * 8 + z]).start()

    @pl.when(y < 4)
    def _():
        sum_c[...] = y_sum(0)

    @pl.when(y >= 4)
    def _():
        sum_c[...] = y_sum(1)

    pw_c[...] = jnp.zeros((3, 48, 128), F32)
    for q in range(3):
        pw_c[q, 0:40] = sum_c[40 * q : 40 * q + 40]
        pw_c[q, 40:41] = sum_c[120 + q : 121 + q]
    for q in range(8):
        rows = [pw_c[k, 5 * q : 5 * q + 8] for k in range(3)]
        ws_c[q] = jnp.concatenate(rows + [extra], axis=0).astype(BF)
        fin_start(0, q)

    pw_r[...] = y_sum(2).reshape(3, 32, 128)
    pack[...] = jnp.zeros((16, 128), F32)
    for q in range(8):
        low = (27 * q) // 8
        for k in range(3):
            pack[5 * k : 5 * k + 5] = pw_r[k, low : low + 5]
        ws_r[q] = pack[...].astype(BF)
        fin_start(1, q)

    def fin_sum(n):
        src, dst = ((ws_c, land_c), (ws_r, land_r))[n]
        total = jnp.zeros(dst.shape[1:], F32)
        for k in range(8):
            pltpu.make_async_copy(src.at[0], dst.at[k], fin_r.at[n * 8 + k]).wait()
            total += dst[k].astype(F32)
        return total

    flat_c[...] = jnp.zeros((24, 128), F32)
    flat_r[...] = jnp.zeros((24, 128), F32)
    total = fin_sum(0)
    og_ref[...] = total[24:26] + total[26:28]
    for k in range(3):
        for u in range(6):
            flat_c[3 * u + k : 3 * u + k + 1] = total[8 * k + u : 8 * k + u + 1]

    def cut(flat, off):
        lane = lax.broadcasted_iota(jnp.int32, (16, 128), 1)
        m, s = off // 128, off % 128
        turn = (128 - s) % 128
        one = pltpu.roll(flat[pl.ds(m, 16)], turn, 1)
        two = pltpu.roll(flat[pl.ds(m + 1, 16)], turn, 1)
        return jnp.where(lane < 128 - s, one, two)

    oc_ref[...] = cut(flat_c, 192 * (r % 2) + 24 * c)

    for p in range(3):
        y_wait_send(p)
    for n in range(2):
        for q in range(8):
            remote_one, own = fin_copy(n, q)

            @pl.when(jnp.logical_not(own))
            def _():
                remote_one.wait_send()

    total = fin_sum(1)
    for k in range(3):
        for u in range(5):
            flat_r[3 * u + k : 3 * u + k + 1] = total[5 * k + u : 5 * k + u + 1]
    or_ref[...] = cut(flat_r, 1296 * c - 384 * ((27 * c) // 8))


def hand_over(gi, oc, orr, og, gi_out, oc_out, or_out, og_out, sem):
    pairs = ((gi, gi_out), (oc, oc_out), (orr, or_out), (og, og_out))
    copies = [pltpu.make_async_copy(a, b, sem.at[n]) for n, (a, b) in enumerate(pairs)]
    for copy in copies:
        copy.start()
    for copy in copies:
        copy.wait()


def local(latent, cotangent, resample_weight, conv_weight, norm_gain):
    vm = pl.BlockSpec(memory_space=pltpu.VMEM)
    far = pl.BlockSpec(memory_space=pltpu.HBM)
    consts = selectors()
    dma, V = pltpu.SemaphoreType.DMA, pltpu.VMEM

    def reduce_buffers(n, tms):
        return [
            V((4, tms, n, 128), BF), V((4, tms, n, 128), BF), V((6, tms // 2, n, 128), BF),
            V((6, tms // 2, n, 128), BF), V((tms, n, 128), F32),
        ]

    scratch = [V(a.shape, BF) for a in consts]
    scratch += [
        V((3, 2, 8, 384), BF), V((1, 192), F32), V((3, 3, 192, 384), BF), V((3, 3, 3, 192, 192), BF),
        V((3, 5, 6, 16, 192), BF), V((3, 4, 16, 384), BF), V((3, 4, 16, 384), BF),
        V((2, 3, 16, 576), BF), V((2, 6, 16, 576), BF), V((64, 192), BF), V((2, 32, 192), BF),
        V((3, 3, 6, 16, 384), BF), V((3, 3, 6, 16, 384), BF),
        V((3, 6, 16, 192), BF), V((3, 3, 6, 16, 192), BF),
        V((3, 2592 + 48, 128), F32), V((3, 1728 + 32, 128), F32),
        V((2, 8, 128), F32), V((4, 8, 128), F32), V((8, 8, 128), F32),
        V((128, 128), F32), V((3, 48, 128), F32), V((3, 32, 128), F32),
        V((8, 32, 128), BF), V((8, 16, 128), BF), V((8, 32, 128), BF), V((8, 16, 128), BF),
        V((16, 128), F32), V((24, 128), F32), V((24, 128), F32),
        dma((17,)), dma((23,)), dma((23,)), dma((12,)), dma((12,)), dma((18,)), dma((18,)), dma((16,)), dma((16,)),
        dma((16,)), dma((16,)), dma((1,)), dma((1,)), dma((3,)), dma((3,)), dma((7,)), dma((7,)),
        *reduce_buffers(128, 4), *reduce_buffers(128, 4), *reduce_buffers(96, 8),
        V((4, 128, 128), BF), V((4, 128, 128), BF), V((8, 96, 128), BF), V((8, 128, 128), BF), V((8, 96, 128), BF),
    ]
    gi, oc, orr, og = pl.pallas_call(
        kernel,
        out_shape=[
            jax.ShapeDtypeStruct((3, 2, 8, 384), BF),
            jax.ShapeDtypeStruct((16, 128), F32),
            jax.ShapeDtypeStruct((16, 128), F32),
            jax.ShapeDtypeStruct((2, 128), F32),
        ],
        in_specs=[far] * (5 + len(consts)),
        out_specs=[vm] * 4,
        scratch_shapes=scratch,
        compiler_params=pltpu.CompilerParams(
            collective_id=0, has_side_effects=True, vmem_limit_bytes=56 * 2**20
        ),
        cost_estimate=pl.CostEstimate(flops=1_600_000_000, bytes_accessed=5_000_000, transcendentals=40_000),
    )(latent, cotangent, norm_gain.reshape(1, 192), jnp.swapaxes(resample_weight, 2, 3), conv_weight, *consts)
    shapes = [jax.ShapeDtypeStruct(a.shape, a.dtype) for a in (gi, oc, orr, og)]
    gi, oc, orr, og = pl.pallas_call(
        hand_over, out_shape=shapes, in_specs=[far] * 4, out_specs=[far] * 4, scratch_shapes=[dma((4,))]
    )(gi, oc, orr, og)
    return gi, orr.reshape(-1)[:1296], oc.reshape(-1)[:1944], og.reshape(-1)[:192]


def solution(mesh):
    in_specs = (P("tm", "rows", "cols", None), P("tm", "rows", "cols", None), P(), P(), P())
    out_specs = (
        P("tm", "rows", "cols", None),
        P(("tm", "rows", "cols")),
        P(("tm", "rows", "cols")),
        P(),
    )
    return jax.shard_map(local, mesh=mesh, in_specs=in_specs, out_specs=out_specs, check_vma=False)
```

time: 84 us -> 70 us (0.83)
  the two profiles are of different devices: /device:TPU:6 before, /device:TPU:57 now
where the time goes in v2:
time: 70 us; the launch traced here: 69.3 us
  Pallas kernels  68.7 us (98%)
    pallas_call x1, Pallas kernels, local(): pl.pallas_call(kernel, out_shape=[jax.ShapeDtypeStruct((3, 2, 8, 384), BF...  65.9 us
    pallas_call x1, Pallas kernels, local(): pl.pallas_call(hand_over, out_shape=shapes, in_specs=[far] * 4, out_specs...  2.78 us

profile of v2, /device:TPU:57, one launch (start us, length us, event | category | flops | bytes accessed | tf_op | source)
XLA Modules:
  0.0 69.3 jit_solution(15713784555912277227)
XLA Ops:
  0.6 65.9 %shard_map.192 = (bf16[3,2,8,384]{3,2,1,0:T(8,128)(2,1)}, f32[16,128]{1,0:T(8,128)}, f32[16,128]{1,0:T(8,128)}, f32[2,128]{1,0:T(2,128)}) custom-call(bf16[3,2,8,384]{3,2,1,0:T(8,128)(2,1)} %refs_0_.1, bf16[3,4,16,192]{3,2,1,0:T(8,128)(2,1)} %refs_1_.1, f32[1,192]{1,0:T(1,128)} %bitcast.11, bf16[3,3,192,384]{3,2,1,0:T(8,128)(2,1)} %bitcast.8, ...), custom_call_target="tpu_custom_call" | custom-call | flops 1600000000 | bytes 5000000 | tf_op jit(solution)/shard_map/pallas_call | solution.py:634
  66.5 2.8 %shard_map.193 = (bf16[3,2,8,384]{3,2,1,0:T(8,128)(2,1)}, f32[16,128]{1,0:T(8,128)}, f32[16,128]{1,0:T(8,128)}, f32[2,128]{1,0:T(2,128)}) custom-call(bf16[3,2,8,384]{3,2,1,0:T(8,128)(2,1)} %get-tuple-element.12.gi, f32[16,128]{1,0:T(8,128)} %get-tuple-element.13.oc, f32[16,128]{1,0:T(8,128)} %get-tuple-element.14.orr, f32[2,128]{1,0:T(2,128)} %get-tuple-element.15.og), custom_call_target="tpu_custom_call" | custom-call | tf_op jit(solution)/shard_map/pallas_call | solution.py:651

commit v3 on v2

--- a/solution.py
+++ b/solution.py
@@ -30,14 +30,9 @@
         even_192[u, 2 * u] = even_192[96 + u, 2 * u + 1] = 1
     for u in range(192):
         even_384[2 * u, u] = even_384[2 * u + 1, 192 + u] = 1
-    lift, lift_rim = zeros(3, 96, 64), zeros(2, 3, 96, 48)
-    cot, cot_rim = zeros(2, 96, 96), zeros(2, 5, 96, 96)
+    lift, lift_rim = zeros(3, 96, 64), zeros(2, 3, 96, 16)
+    cot, cot_rim = zeros(2, 96, 96), zeros(2, 5, 96, 32)
     pair, pair_rim = zeros(3, 96, 96), zeros(2, 3, 96, 32)
-
-    def slot(at, last, frame, late):
-        kind = 1 if at == 0 else 2 if at == last else 0
-        row = frame if kind else frame * (last - 1) + at - 1
-        return (kind + 3 * late) * 16 + row
 
     for row in range(6):
         for c in range(16):
@@ -53,21 +48,37 @@
                 else:
                     side = j // 2
                     for f in range(5):
-                        cot_rim[side, f, out, slot(row, 5, f % 3, f // 3)] = 1
+                        cot_rim[side, f, out, f * 6 + row] = 1
                     for f in range(3):
-                        lift_rim[side, f, out, slot(low[row], 3, f, 0)] = 1
+                        lift_rim[side, f, out, f * 4 + low[row]] = 1
                         pair_rim[side, f, par, f * 6 + row] = 1
-    edge_cot, edge_low, edge_delta = zeros(96, 192), zeros(96, 96), zeros(64, 288)
+    edge_delta, edges, rims = zeros(64, 288), zeros(192, 672), zeros(112, 128)
     for side, col in ((0, 0), (1, 15)):
         for n in range(18):
             edge_delta[side * 32 + n, n * 16 + col] = 1
-        for t in range(3):
-            for rows, edge in ((4, edge_cot), (2, edge_low)):
-                for row in range(rows):
-                    edge[side * 48 + t * rows + row, (t * rows + row) * 16 + col] = 1
-                edge[side * 48 + 16 + t, t * rows * 16 + col] = 1
-                edge[side * 48 + 32 + t, (t * rows + rows - 1) * 16 + col] = 1
-    parts = (widen, even_192, even_384, lift, lift_rim, cot, cot_rim, pair, pair_rim, edge_cot, edge_low, edge_delta)
+        for chunks, rows, src, at, corner in ((3, 2, 0, 0, 0), (2, 4, 288, 18, 9)):
+            for q in range(chunks):
+                for t in range(3):
+                    here = src + q * rows * 48 + t * rows * 16 + col
+                    for row in range(rows):
+                        edges[side * 96 + at + (q * 3 + t) * rows + row, here + row * 16] = 1
+                        if rows == 4 and t < 2:
+                            edges[side * 96 + 80 + q * 8 + t * 4 + row, here + row * 16] = 1
+                    edges[side * 96 + 48 + corner + q * 3 + t, here] = 1
+                    edges[side * 96 + 64 + corner + q * 3 + t, here + (rows - 1) * 16] = 1
+    for t in range(3):
+        for q in range(3):
+            rims[q * 16 + t * 4, 48 + q * 3 + t] = rims[q * 16 + t * 4 + 3, 64 + q * 3 + t] = 1
+            for row in range(2):
+                rims[q * 16 + t * 4 + 1 + row, q * 6 + t * 2 + row] = 1
+        for q in range(2):
+            for f, base, up, down in ((t, 18 + q * 12, 48, 64), (t + 3, 80 + q * 8, 96, 112)):
+                if f < 5:
+                    at = 48 + q * 32 + f * 6
+                    rims[at, up + 9 + q * 3 + t] = rims[at + 5, down + 9 + q * 3 + t] = 1
+                    for row in range(4):
+                        rims[at + 1 + row, base + t * 4 + row] = 1
+    parts = (widen, edges, rims, even_192, even_384, lift, lift_rim, cot, cot_rim, pair, pair_rim, edge_delta)
     return [jnp.asarray(p, BF) for p in parts]
 
 
@@ -87,16 +98,16 @@
     (latent_hbm, cot_hbm, gain_hbm, wr_hbm, wc_hbm), refs = refs[:5], refs[5:]
     const_hbm, (gi_ref, oc_ref, or_ref, og_ref), refs = refs[:12], refs[12:16], refs[16:]
     consts, refs = refs[:12], refs[12:]
-    (widen, even_192, even_384, lift, lift_rim, cot, cot_rim, pair, pair_rim, edge_cot, edge_low, edge_delta) = consts
+    (widen, edges, rims, even_192, even_384, lift, lift_rim, cot, cot_rim, pair, pair_rim, edge_delta) = consts
     (
         latv, gain_v, wr, wc, sc, lc, lcp, hs, rim, hs_d, rim_d, sl, slp, xd, sd, fc, fr,
         g_core, g_x, g_y, sum_c, pw_c, pw_r, ws_c, ws_r, land_c, land_r, pack, flat_c, flat_r,
         load_sem, ssem, rsem, core_s, core_r, x_s, x_r, y_s, y_r, fin_s, fin_r,
         gc_s, gc_r, gx_s, gx_r, gy_s, gy_r,
     ), refs = refs[:47], refs[47:]
-    bufs = [refs[5 * p : 5 * p + 5] for p in range(3)]
-    yr_c, yr_r = refs[18:20]
-    y_bufs = [(refs[15], yr_c), (refs[16], yr_c), (refs[17], yr_r)]
+    bufs = [refs[5 * p : 5 * p + 5] for p in range(4)]
+    yr_c, yr_r = refs[24:26]
+    y_bufs = [(refs[20 + p], yr_c if p < 2 else yr_r) for p in range(4)]
 
     y, r, c = lax.axis_index("tm"), lax.axis_index("rows"), lax.axis_index("cols")
     h, zl = r % 2, r // 2
@@ -110,6 +121,13 @@
 
     def peer_x(o):
         return (y, r, zh * 4 + (x + o) % 4)
+
+    f3, f2, late = pl.ds(0, 3), pl.ds(0, 2), pl.ds(3, 2)
+    targets = [(latent_hbm, latv), (cot_hbm, sc.at[1, f3, pl.ds(1, 4)])]
+    targets += list(zip(const_hbm, consts)) + [(gain_hbm, gain_v), (wr_hbm, wr), (wc_hbm, wc)]
+    loads = [pltpu.make_async_copy(a, b, load_sem.at[n]) for n, (a, b) in enumerate(targets)]
+    for copy in loads[:4]:
+        copy.start()
 
     bar = pltpu.get_barrier_semaphore()
     sources = [dev(dy, dr, dc) for dc in (1, -1, 0) for dr in (-1, 0, 1) for dy in (0, 1) if (dy, dr, dc) != (0, 0, 0)]
@@ -124,80 +142,102 @@
             pl.semaphore_signal(bar, inc=1, device_id=src, device_id_type=MESH)
 
     mine = jnp.where(r == 4 * h + x, 1, 0)
-
-    f3, f2, late = pl.ds(0, 3), pl.ds(0, 2), pl.ds(3, 2)
-    targets = [(latent_hbm, latv), (cot_hbm, sc.at[1, f3, pl.ds(1, 4)]), (gain_hbm, gain_v)]
-    targets += [(a, b) for a, b in zip(const_hbm, consts)] + [(wr_hbm, wr), (wc_hbm, wc)]
-    loads = [pltpu.make_async_copy(a, b, load_sem.at[n]) for n, (a, b) in enumerate(targets)]
-    for copy in loads:
+    for copy in loads[4:]:
         copy.start()
-    for copy in loads[:-2]:
+    for copy in loads[:4]:
         copy.wait()
 
     own_low = latv[...].astype(F32).reshape(48, 384).astype(BF)
     own_low = mm(widen[...], own_low).astype(BF)
     lc[:, 1:3] = own_low.reshape(3, 2, 16, 384)
-    hs[:, :, :, 0:384] = mm(edge_low[...], own_low).astype(BF).reshape(2, 3, 16, 384)
     own_cot = sc[1, 0:3, 1:5].reshape(192, 192)
-    hs[:, :, :, 384:576] = mm(edge_cot[...], own_cot).astype(BF).reshape(2, 3, 16, 192)
+    chunks = [own_low[:, 0:128], own_low[:, 128:256], own_low[:, 256:384], own_cot[:, 0:128]]
+    chunks += [jnp.concatenate([own_cot[:, 128:192], jnp.zeros((192, 64), BF)], axis=1)]
+    hs[...] = mm(edges[...], jnp.concatenate(chunks, axis=0)).astype(BF)
 
     pl.semaphore_wait(bar, len(sources) + 8 - mine)
 
-    def remote(src, dst, n, to):
-        return pltpu.make_async_remote_copy(
-            src_ref=src, dst_ref=dst, send_sem=ssem.at[n], recv_sem=rsem.at[n],
-            device_id=to, device_id_type=MESH,
-        )
+    def inside(dy, dr, dc):
+        ok = y >= 0
+        for at, d in ((y, dy), (r, dr), (c, dc)):
+            if d:
+                ok = jnp.logical_and(ok, at < 7 if d > 0 else at > 0)
+        return ok
+
+    class Halo:
+        def __init__(self, src, dst, n, *to):
+            self.to, self.back = inside(*to), inside(*[-d for d in to])
+            self.copy = pltpu.make_async_remote_copy(
+                src_ref=src, dst_ref=dst, send_sem=ssem.at[n], recv_sem=rsem.at[n],
+                device_id=dev(*to), device_id_type=MESH,
+            )
+
+        def start(self):
+            pl.when(self.to)(self.copy.start)
+
+        def wait(self):
+            pl.when(self.to)(self.copy.wait_send)
+            pl.when(self.back)(self.copy.wait_recv)
 
     halo = []
     for s, dc in ((0, -1), (1, 1)):
-        for n, (tile, dy, dr) in enumerate(((0, 0, 0), (2, 0, 1), (1, 0, -1), (0, -1, 0), (2, -1, 1), (1, -1, -1))):
-            halo.append(remote(hs.at[s, tile], rim.at[1 - s, n], 11 + 6 * s + n, dev(dy, dr, dc)))
+        tiles = ((0, 48, 0, 0, 0), (64, 16, 48, 0, 1), (48, 16, 64, 0, -1), (80, 16, 80, -1, 0), (64, 16, 96, -1, 1), (48, 16, 112, -1, -1))
+        for n, (src, rows, dst, dy, dr) in enumerate(tiles):
+            halo.append(Halo(hs.at[pl.ds(96 * s + src, rows)], rim.at[1 - s, pl.ds(dst, rows)], 11 + 6 * s + n, dy, dr, dc))
     halo += [
-        remote(lc.at[f3, 1], lc.at[f3, 3], 5, dev(0, -1)),
-        remote(lc.at[f3, 2], lc.at[f3, 0], 6, dev(0, 1)),
-        remote(sc.at[1, f3, 1], sc.at[1, f3, 5], 0, dev(0, -1)),
-        remote(sc.at[1, f3, 4], sc.at[1, f3, 0], 1, dev(0, 1)),
-        remote(sc.at[1, f2, pl.ds(1, 4)], sc.at[1, late, pl.ds(1, 4)], 2, dev(-1, 0)),
-        remote(sc.at[1, f2, 1], sc.at[1, late, 5], 3, dev(-1, -1)),
-        remote(sc.at[1, f2, 4], sc.at[1, late, 0], 4, dev(-1, 1)),
+        Halo(lc.at[f3, 1], lc.at[f3, 3], 5, 0, -1, 0),
+        Halo(lc.at[f3, 2], lc.at[f3, 0], 6, 0, 1, 0),
+        Halo(sc.at[1, f3, 1], sc.at[1, f3, 5], 0, 0, -1, 0),
+        Halo(sc.at[1, f3, 4], sc.at[1, f3, 0], 1, 0, 1, 0),
+        Halo(sc.at[1, f2, pl.ds(1, 4)], sc.at[1, late, pl.ds(1, 4)], 2, -1, 0, 0),
+        Halo(sc.at[1, f2, 1], sc.at[1, late, 5], 3, -1, -1, 0),
+        Halo(sc.at[1, f2, 4], sc.at[1, late, 0], 4, -1, 1, 0),
     ]
     for copy in halo:
         copy.start()
-    for copy in loads[-2:]:
+
+    @pl.when(r == 0)
+    def _():
+        sc[1, :, 0] = jnp.zeros((5, 16, 192), BF)
+        lc[:, 0] = jnp.zeros((3, 16, 384), BF)
+        xd[:, 0] = jnp.zeros((3, 16, 192), BF)
+        for n in (48, 96):
+            rim[:, n : n + 16] = jnp.zeros((2, 16, 128), BF)
+
+    @pl.when(r == 7)
+    def _():
+        sc[1, :, 5] = jnp.zeros((5, 16, 192), BF)
+        lc[:, 3] = jnp.zeros((3, 16, 384), BF)
+        xd[:, 5] = jnp.zeros((3, 16, 192), BF)
+        for n in (64, 112):
+            rim[:, n : n + 16] = jnp.zeros((2, 16, 128), BF)
+
+    @pl.when(y == 7)
+    def _():
+        sc[1, 3:5] = jnp.zeros((2, 6, 16, 192), BF)
+        rim[:, 80:128] = jnp.zeros((2, 48, 128), BF)
+
+    @pl.when(c == 0)
+    def _():
+        rim[0] = jnp.zeros((128, 128), BF)
+        rim_d[0] = jnp.zeros((32, 192), BF)
+
+    @pl.when(c == 7)
+    def _():
+        rim[1] = jnp.zeros((128, 128), BF)
+        rim_d[1] = jnp.zeros((32, 192), BF)
+
+    for copy in loads[4:]:
         copy.wait()
     for copy in halo:
         copy.wait()
 
-    @pl.when(r == 0)
-    def _():
-        sc[1, :, 0] = jnp.zeros((5, 16, 192), BF)
-        lc[:, 0] = jnp.zeros((3, 16, 384), BF)
-        for n in (1, 4):
-            rim[:, n] = jnp.zeros((2, 16, 576), BF)
-
-    @pl.when(r == 7)
-    def _():
-        sc[1, :, 5] = jnp.zeros((5, 16, 192), BF)
-        lc[:, 3] = jnp.zeros((3, 16, 384), BF)
-        for n in (2, 5):
-            rim[:, n] = jnp.zeros((2, 16, 576), BF)
-
-    @pl.when(y == 7)
-    def _():
-        sc[1, 3:5] = jnp.zeros((2, 6, 16, 192), BF)
-        rim[:, 3:6] = jnp.zeros((2, 3, 16, 576), BF)
-
-    @pl.when(c == 0)
-    def _():
-        rim[0] = jnp.zeros((6, 16, 576), BF)
-
-    @pl.when(c == 7)
-    def _():
-        rim[1] = jnp.zeros((6, 16, 576), BF)
-
+    rim_l, rim_c = [], []
+    for s in range(2):
+        near = mm(rims[...], rim[s]).astype(BF)
+        rim_l.append(jnp.concatenate([near[0:16], near[16:32], near[32:48]], axis=1))
+        rim_c.append(jnp.concatenate([near[48:80], near[80:112, 0:64]], axis=1))
     lcp[...] = mm(lc[...].reshape(192, 384), even_384[...]).astype(BF).reshape(3, 4, 16, 384)
-    rim_l = [rim[s, 0:3, :, 0:384].reshape(48, 384) for s in range(2)]
     rim_p = [mm(rim_l[s], even_384[...]).astype(BF) for s in range(2)]
     for t in range(3):
         here = lc[t].reshape(64, 384)
@@ -227,7 +267,7 @@
     for f in range(5):
         here = sc[1, f].reshape(96, 192)
         for s in range(2):
-            moved = mm(cot[s], here) + mm(cot_rim[s, f], rim[s, :, :, 384:576].reshape(96, 192))
+            moved = mm(cot[s], here) + mm(cot_rim[s, f], rim_c[s])
             sc[2 * s, f] = moved.astype(BF).reshape(6, 16, 192)
 
     def cot_view(a, i, j):
@@ -258,7 +298,7 @@
         at = 27 * (t * 8 + 4 * hh + i)
         return jnp.concatenate([fr[q, pl.ds(at, 32)] for q in range(3)], axis=0)
 
-    parts = [(block_c, 0, 4), (block_c, 4, 8), (block_r, 0, 8)]
+    parts = [(block_c, 0, 4), (block_c, 4, 8), (block_r, 0, 4), (block_r, 4, 8)]
 
     def core_copy(p, o):
         bs, br = bufs[p][:2]
@@ -329,10 +369,10 @@
 
     def y_copy(p, t):
         ys, yr = y_bufs[p]
-        n = (0, 4, 8)[p] + t - parts[p][1]
+        n = p * 4 + t - parts[p][1]
         return pltpu.make_async_remote_copy(
             src_ref=ys.at[t - parts[p][1]], dst_ref=yr.at[y], send_sem=y_s.at[n],
-            recv_sem=y_r.at[min(p, 2) // 2 * 8 + y], device_id=(t, r, c), device_id_type=MESH)
+            recv_sem=y_r.at[p // 2 * 8 + y], device_id=(t, r, c), device_id_type=MESH)
 
     def y_send(p):
         _, lo, hi = parts[p]
@@ -370,7 +410,7 @@
         total = ac[y - lo]
         for o in range(1, 8):
             k = (y + o) % 8
-            pltpu.make_async_copy(yr.at[k], yr.at[k], y_r.at[min(p, 2) // 2 * 8 + k]).wait()
+            pltpu.make_async_copy(yr.at[k], yr.at[k], y_r.at[p // 2 * 8 + k]).wait()
             total += yr[k].astype(F32)
         return total
 
@@ -398,8 +438,8 @@
     ).astype(BF)
     xd[:, 1:5] = delta.reshape(3, 4, 16, 192)
     rows_d = [
-        remote(xd.at[f3, 1], xd.at[f3, 5], 7, dev(0, -1)),
-        remote(xd.at[f3, 4], xd.at[f3, 0], 8, dev(0, 1)),
+        Halo(xd.at[f3, 1], xd.at[f3, 5], 7, 0, -1, 0),
+        Halo(xd.at[f3, 4], xd.at[f3, 0], 8, 0, 1, 0),
     ]
     for copy in rows_d:
         copy.start()
@@ -423,26 +463,20 @@
             planes(mm_tn(view, delta), 192, fr, at)
         return carry
 
-    lax.fori_loop(0, 3, lift_taps, 0)
+    lax.fori_loop(0, 2, lift_taps, 0)
     core_send(2)
     x_second(1)
+    lax.fori_loop(2, 3, lift_taps, 0)
     x_first(2)
+    core_send(3)
 
     for copy in rows_d:
         copy.wait()
 
-    @pl.when(r == 0)
-    def _():
-        xd[:, 0] = jnp.zeros((3, 16, 192), BF)
-
-    @pl.when(r == 7)
-    def _():
-        xd[:, 5] = jnp.zeros((3, 16, 192), BF)
-
     hs_d[...] = mm(edge_delta[...], xd[...].reshape(288, 192)).astype(BF)
     cols_d = [
-        remote(hs_d.at[pl.ds(0, 32)], rim_d.at[1], 9, dev(0, 0, -1)),
-        remote(hs_d.at[pl.ds(32, 32)], rim_d.at[0], 10, dev(0, 0, 1)),
+        Halo(hs_d.at[pl.ds(0, 32)], rim_d.at[1], 9, 0, 0, -1),
+        Halo(hs_d.at[pl.ds(32, 32)], rim_d.at[0], 10, 0, 0, 1),
     ]
     for copy in cols_d:
         copy.start()
@@ -453,8 +487,10 @@
     for copy in g2:
         copy.start()
 
+    x_first(3)
+    x_second(2)
     y_send(0)
-    x_second(2)
+    x_second(3)
 
     for copy in g2:
         copy.wait()
@@ -464,17 +500,10 @@
         copy.start()
 
     y_send(1)
+    y_send(2)
 
     for copy in cols_d:
         copy.wait()
-
-    @pl.when(c == 0)
-    def _():
-        rim_d[0] = jnp.zeros((32, 192), BF)
-
-    @pl.when(c == 7)
-    def _():
-        rim_d[1] = jnp.zeros((32, 192), BF)
 
     for t in range(3):
         here = xd[t].reshape(96, 192)
@@ -492,7 +521,7 @@
     lifted_grad = lax.fori_loop(0, 3, unlift, jnp.zeros((192, 384), F32))
     gi_ref[...] = lifted_grad.reshape(3, 2, 4, 8, 384).sum(axis=2).astype(BF)
 
-    y_send(2)
+    y_send(3)
 
     for copy in g3:
         copy.wait()
@@ -541,7 +570,14 @@
         ws_c[q] = jnp.concatenate(rows + [extra], axis=0).astype(BF)
         fin_start(0, q)
 
-    pw_r[...] = y_sum(2).reshape(3, 32, 128)
+    @pl.when(y < 4)
+    def _():
+        pw_r[...] = y_sum(2).reshape(3, 32, 128)
+
+    @pl.when(y >= 4)
+    def _():
+        pw_r[...] = y_sum(3).reshape(3, 32, 128)
+
     pack[...] = jnp.zeros((16, 128), F32)
     for q in range(8):
         low = (27 * q) // 8
@@ -576,7 +612,7 @@
 
     oc_ref[...] = cut(flat_c, 192 * (r % 2) + 24 * c)
 
-    for p in range(3):
+    for p in range(4):
         y_wait_send(p)
     for n in range(2):
         for q in range(8):
@@ -618,7 +654,7 @@
     scratch += [
         V((3, 2, 8, 384), BF), V((1, 192), F32), V((3, 3, 192, 384), BF), V((3, 3, 3, 192, 192), BF),
         V((3, 5, 6, 16, 192), BF), V((3, 4, 16, 384), BF), V((3, 4, 16, 384), BF),
-        V((2, 3, 16, 576), BF), V((2, 6, 16, 576), BF), V((64, 192), BF), V((2, 32, 192), BF),
+        V((192, 128), BF), V((2, 128, 128), BF), V((64, 192), BF), V((2, 32, 192), BF),
         V((3, 3, 6, 16, 384), BF), V((3, 3, 6, 16, 384), BF),
         V((3, 6, 16, 192), BF), V((3, 3, 6, 16, 192), BF),
         V((3, 2592 + 48, 128), F32), V((3, 1728 + 32, 128), F32),
@@ -626,10 +662,10 @@
         V((128, 128), F32), V((3, 48, 128), F32), V((3, 32, 128), F32),
         V((8, 32, 128), BF), V((8, 16, 128), BF), V((8, 32, 128), BF), V((8, 16, 128), BF),
         V((16, 128), F32), V((24, 128), F32), V((24, 128), F32),
-        dma((17,)), dma((23,)), dma((23,)), dma((12,)), dma((12,)), dma((18,)), dma((18,)), dma((16,)), dma((16,)),
+        dma((17,)), dma((23,)), dma((23,)), dma((16,)), dma((16,)), dma((24,)), dma((24,)), dma((16,)), dma((16,)),
         dma((16,)), dma((16,)), dma((1,)), dma((1,)), dma((3,)), dma((3,)), dma((7,)), dma((7,)),
-        *reduce_buffers(128, 4), *reduce_buffers(128, 4), *reduce_buffers(96, 8),
-        V((4, 128, 128), BF), V((4, 128, 128), BF), V((8, 96, 128), BF), V((8, 128, 128), BF), V((8, 96, 128), BF),
+        *reduce_buffers(128, 4), *reduce_buffers(128, 4), *reduce_buffers(96, 4), *reduce_buffers(96, 4),
+        V((4, 128, 128), BF), V((4, 128, 128), BF), V((4, 96, 128), BF), V((4, 96, 128), BF), V((8, 128, 128), BF), V((8, 96, 128), BF),
     ]
     gi, oc, orr, og = pl.pallas_call(
         kernel,

time: 70 us -> 64.2 us (0.917)
  Pallas kernels: 68.7 us -> 62.4 us
    pallas_call x1, Pallas kernels: 65.9 us -> 59.7 us  [local(): pl.pallas_call(kernel, out_shape=[jax.ShapeDtypeStruct((3, 2, 8, 384), BF...]
where the time goes in v3:
time: 64.2 us; the launch traced here: 63.1 us
  Pallas kernels  62.4 us (97%)
    pallas_call x1, Pallas kernels, local(): pl.pallas_call(kernel, out_shape=[jax.ShapeDtypeStruct((3, 2, 8, 384), BF...  59.7 us
    pallas_call x1, Pallas kernels, local(): pl.pallas_call(hand_over, out_shape=shapes, in_specs=[far] * 4, out_specs...  2.78 us

profile of v3, /device:TPU:57, one launch (start us, length us, event | category | flops | bytes accessed | tf_op | source)
XLA Modules:
  0.0 63.1 jit_solution(1804964479776828966)
XLA Ops:
  0.6 59.7 %shard_map.192 = (bf16[3,2,8,384]{3,2,1,0:T(8,128)(2,1)}, f32[16,128]{1,0:T(8,128)}, f32[16,128]{1,0:T(8,128)}, f32[2,128]{1,0:T(2,128)}) custom-call(bf16[3,2,8,384]{3,2,1,0:T(8,128)(2,1)} %refs_0_.1, bf16[3,4,16,192]{3,2,1,0:T(8,128)(2,1)} %refs_1_.1, f32[1,192]{1,0:T(1,128)} %bitcast.11, bf16[3,3,192,384]{3,2,1,0:T(8,128)(2,1)} %bitcast.8, ...), custom_call_target="tpu_custom_call" | custom-call | flops 1600000000 | bytes 5000000 | tf_op jit(solution)/shard_map/pallas_call | solution.py:670
  60.3 2.8 %shard_map.193 = (bf16[3,2,8,384]{3,2,1,0:T(8,128)(2,1)}, f32[16,128]{1,0:T(8,128)}, f32[16,128]{1,0:T(8,128)}, f32[2,128]{1,0:T(2,128)}) custom-call(bf16[3,2,8,384]{3,2,1,0:T(8,128)(2,1)} %get-tuple-element.12.gi, f32[16,128]{1,0:T(8,128)} %get-tuple-element.13.oc, f32[16,128]{1,0:T(8,128)} %get-tuple-element.14.orr, f32[2,128]{1,0:T(2,128)} %get-tuple-element.15.og), custom_call_target="tpu_custom_call" | custom-call | tf_op jit(solution)/shard_map/pallas_call | solution.py:687

commit v4 on v3

--- a/solution.py
+++ b/solution.py
@@ -52,20 +52,21 @@
                     for f in range(3):
                         lift_rim[side, f, out, f * 4 + low[row]] = 1
                         pair_rim[side, f, par, f * 6 + row] = 1
-    edge_delta, edges, rims = zeros(64, 288), zeros(192, 672), zeros(112, 128)
+    edge_delta, edges, rims = zeros(64, 288), zeros(192, 528), zeros(112, 128)
     for side, col in ((0, 0), (1, 15)):
         for n in range(18):
             edge_delta[side * 32 + n, n * 16 + col] = 1
-        for chunks, rows, src, at, corner in ((3, 2, 0, 0, 0), (2, 4, 288, 18, 9)):
+        for chunks, rows, src, at, corner in ((3, 2, 0, 0, 0), (2, 4, 144, 18, 9)):
+            wide, at_col = (8, col // 2) if rows == 2 else (16, col)
             for q in range(chunks):
                 for t in range(3):
-                    here = src + q * rows * 48 + t * rows * 16 + col
+                    here = src + (q * 3 + t) * rows * wide + at_col
                     for row in range(rows):
-                        edges[side * 96 + at + (q * 3 + t) * rows + row, here + row * 16] = 1
+                        edges[side * 96 + at + (q * 3 + t) * rows + row, here + row * wide] = 1
                         if rows == 4 and t < 2:
-                            edges[side * 96 + 80 + q * 8 + t * 4 + row, here + row * 16] = 1
+                            edges[side * 96 + 80 + q * 8 + t * 4 + row, here + row * wide] = 1
                     edges[side * 96 + 48 + corner + q * 3 + t, here] = 1
-                    edges[side * 96 + 64 + corner + q * 3 + t, here + (rows - 1) * 16] = 1
+                    edges[side * 96 + 64 + corner + q * 3 + t, here + (rows - 1) * wide] = 1
     for t in range(3):
         for q in range(3):
             rims[q * 16 + t * 4, 48 + q * 3 + t] = rims[q * 16 + t * 4 + 3, 64 + q * 3 + t] = 1
@@ -78,7 +79,7 @@
                     rims[at, up + 9 + q * 3 + t] = rims[at + 5, down + 9 + q * 3 + t] = 1
                     for row in range(4):
                         rims[at + 1 + row, base + t * 4 + row] = 1
-    parts = (widen, edges, rims, even_192, even_384, lift, lift_rim, cot, cot_rim, pair, pair_rim, edge_delta)
+    parts = (edges, even_384, widen, rims, even_192, lift, lift_rim, cot, cot_rim, pair, pair_rim, edge_delta)
     return [jnp.asarray(p, BF) for p in parts]
 
 
@@ -98,16 +99,16 @@
     (latent_hbm, cot_hbm, gain_hbm, wr_hbm, wc_hbm), refs = refs[:5], refs[5:]
     const_hbm, (gi_ref, oc_ref, or_ref, og_ref), refs = refs[:12], refs[12:16], refs[16:]
     consts, refs = refs[:12], refs[12:]
-    (widen, edges, rims, even_192, even_384, lift, lift_rim, cot, cot_rim, pair, pair_rim, edge_delta) = consts
+    (edges, even_384, widen, rims, even_192, lift, lift_rim, cot, cot_rim, pair, pair_rim, edge_delta) = consts
     (
-        latv, gain_v, wr, wc, sc, lc, lcp, hs, rim, hs_d, rim_d, sl, slp, xd, sd, fc, fr,
+        latv, gain_v, wr, wrp, wc, sc, lc, hs, rim, hs_d, rim_d, sl, xd, sd, fc, fr,
         g_core, g_x, g_y, sum_c, pw_c, pw_r, ws_c, ws_r, land_c, land_r, pack, flat_c, flat_r,
         load_sem, ssem, rsem, core_s, core_r, x_s, x_r, y_s, y_r, fin_s, fin_r,
         gc_s, gc_r, gx_s, gx_r, gy_s, gy_r,
-    ), refs = refs[:47], refs[47:]
-    bufs = [refs[5 * p : 5 * p + 5] for p in range(4)]
-    yr_c, yr_r = refs[24:26]
-    y_bufs = [(refs[20 + p], yr_c if p < 2 else yr_r) for p in range(4)]
+    ), refs = refs[:46], refs[46:]
+    bufs = [refs[5 * p : 5 * p + 5] for p in range(5)]
+    yr_c, yr_r = refs[30:32]
+    y_bufs = [(refs[25 + p], yr_c if p < 3 else yr_r) for p in range(5)]
 
     y, r, c = lax.axis_index("tm"), lax.axis_index("rows"), lax.axis_index("cols")
     h, zl = r % 2, r // 2
@@ -126,7 +127,7 @@
     targets = [(latent_hbm, latv), (cot_hbm, sc.at[1, f3, pl.ds(1, 4)])]
     targets += list(zip(const_hbm, consts)) + [(gain_hbm, gain_v), (wr_hbm, wr), (wc_hbm, wc)]
     loads = [pltpu.make_async_copy(a, b, load_sem.at[n]) for n, (a, b) in enumerate(targets)]
-    for copy in loads[:4]:
+    for copy in loads[:5]:
         copy.start()
 
     bar = pltpu.get_barrier_semaphore()
@@ -142,14 +143,10 @@
             pl.semaphore_signal(bar, inc=1, device_id=src, device_id_type=MESH)
 
     mine = jnp.where(r == 4 * h + x, 1, 0)
-    for copy in loads[4:]:
-        copy.start()
     for copy in loads[:4]:
         copy.wait()
 
-    own_low = latv[...].astype(F32).reshape(48, 384).astype(BF)
-    own_low = mm(widen[...], own_low).astype(BF)
-    lc[:, 1:3] = own_low.reshape(3, 2, 16, 384)
+    own_low = mm(latv[...].astype(F32).reshape(48, 384).astype(BF), even_384[...]).astype(BF)
     own_cot = sc[1, 0:3, 1:5].reshape(192, 192)
     chunks = [own_low[:, 0:128], own_low[:, 128:256], own_low[:, 256:384], own_cot[:, 0:128]]
     chunks += [jnp.concatenate([own_cot[:, 128:192], jnp.zeros((192, 64), BF)], axis=1)]
@@ -184,6 +181,10 @@
         tiles = ((0, 48, 0, 0, 0), (64, 16, 48, 0, 1), (48, 16, 64, 0, -1), (80, 16, 80, -1, 0), (64, 16, 96, -1, 1), (48, 16, 112, -1, -1))
         for n, (src, rows, dst, dy, dr) in enumerate(tiles):
             halo.append(Halo(hs.at[pl.ds(96 * s + src, rows)], rim.at[1 - s, pl.ds(dst, rows)], 11 + 6 * s + n, dy, dr, dc))
+    for copy in halo:
+        copy.start()
+    loads[4].wait()
+    lc[:, 1:3] = mm(widen[...], own_low).astype(BF).reshape(3, 2, 16, 384)
     halo += [
         Halo(lc.at[f3, 1], lc.at[f3, 3], 5, 0, -1, 0),
         Halo(lc.at[f3, 2], lc.at[f3, 0], 6, 0, 1, 0),
@@ -193,7 +194,7 @@
         Halo(sc.at[1, f2, 1], sc.at[1, late, 5], 3, -1, -1, 0),
         Halo(sc.at[1, f2, 4], sc.at[1, late, 0], 4, -1, 1, 0),
     ]
-    for copy in halo:
+    for copy in halo[12:] + loads[5:]:
         copy.start()
 
     @pl.when(r == 0)
@@ -227,8 +228,14 @@
         rim[1] = jnp.zeros((128, 128), BF)
         rim_d[1] = jnp.zeros((32, 192), BF)
 
-    for copy in loads[4:]:
+    for copy in loads[5:]:
         copy.wait()
+
+    def reorder(n, carry):
+        wrp[n // 3, n % 3] = mm(wr[n // 3, n % 3], even_384[...]).astype(BF)
+        return carry
+
+    lax.fori_loop(0, 9, reorder, 0)
     for copy in halo:
         copy.wait()
 
@@ -237,22 +244,17 @@
         near = mm(rims[...], rim[s]).astype(BF)
         rim_l.append(jnp.concatenate([near[0:16], near[16:32], near[32:48]], axis=1))
         rim_c.append(jnp.concatenate([near[48:80], near[80:112, 0:64]], axis=1))
-    lcp[...] = mm(lc[...].reshape(192, 384), even_384[...]).astype(BF).reshape(3, 4, 16, 384)
-    rim_p = [mm(rim_l[s], even_384[...]).astype(BF) for s in range(2)]
     for t in range(3):
         here = lc[t].reshape(64, 384)
-        here_p = lcp[t].reshape(64, 384)
         for j in range(3):
-            wide, wide_p = mm(lift[j], here), mm(lift[j], here_p)
+            wide = mm(lift[j], here)
             if j != 1:
                 wide += mm(lift_rim[j // 2, t], rim_l[j // 2])
-                wide_p += mm(lift_rim[j // 2, t], rim_p[j // 2])
             sl[j, t] = wide.astype(BF).reshape(6, 16, 384)
-            slp[j, t] = wide_p.astype(BF).reshape(6, 16, 384)
 
     def fwd(i, total):
         for j in range(3):
-            total += mm_nt(sl[j, :, pl.ds(i, 4)].reshape(192, 384), wr[i, j])
+            total += mm_nt(sl[j, :, pl.ds(i, 4)].reshape(192, 384), wrp[i, j])
         return total
 
     z_float = lax.fori_loop(0, 3, fwd, jnp.zeros((192, 192), F32)).astype(BF).astype(F32)
@@ -278,11 +280,13 @@
         dst[1, pl.ds(at, half)] = jnp.concatenate([both[:half, 128:], both[half:, :64]], axis=1)
         dst[2, pl.ds(at, half)] = both[half:, 64:]
 
+    def conv_tap(n, j):
+        at = (n * 3 + j) * 96
+        planes(mm(hidden_t, cot_view(n // 3, n % 3, j)), 96, fc, at if isinstance(n, int) else pl.multiple_of(at, 96))
+
     def conv_taps(n, carry):
-        a, i = n // 3, n % 3
         for j in range(3):
-            at = pl.multiple_of((n * 3 + j) * 96, 96)
-            planes(mm(hidden_t, cot_view(a, i, j)), 96, fc, at)
+            conv_tap(n, j)
         return carry
 
     lane_row = lax.broadcasted_iota(jnp.int32, (8, 128), 0)
@@ -298,7 +302,14 @@
         at = 27 * (t * 8 + 4 * hh + i)
         return jnp.concatenate([fr[q, pl.ds(at, 32)] for q in range(3)], axis=0)
 
-    parts = [(block_c, 0, 4), (block_c, 4, 8), (block_r, 0, 4), (block_r, 4, 8)]
+    parts = [
+        (block_c, (0, 1)), (block_c, (3, 6)), (block_c, (2, 4, 5, 7)),
+        (block_r, (0, 2, 4, 6)), (block_r, (1, 3, 5, 7)),
+    ]
+
+    def halves(p):
+        tms = list(enumerate(parts[p][1]))
+        return tms[: len(tms) // 2], tms[len(tms) // 2 :]
 
     def core_copy(p, o):
         bs, br = bufs[p][:2]
@@ -314,112 +325,101 @@
             recv_sem=x_r.at[p * 6 + m], device_id=peer_x(1 if m % 2 == 0 else 3), device_id_type=MESH)
 
     def core_send(p):
-        block, lo, hi = parts[p]
+        block, tms = parts[p]
         bs = bufs[p][0]
         for o in (2, 1, 3, 0):
             i = (x + o) % 4
-
-            def fill(t, carry):
-                bs[i, t - lo] = block(1 - h, i, t).astype(BF)
-                return carry
-
-            lax.fori_loop(lo, hi, fill, 0)
+            for n, t in enumerate(tms):
+                bs[i, n] = block(1 - h, i, t).astype(BF)
             core_copy(p, o).start()
 
-    def x_fill(p, m, i, first, last, relayed):
-        block, lo, _ = parts[p]
+    def x_fill(p, m, i, half, relayed):
+        block = parts[p][0]
         _, br, xs, xr = bufs[p][:4]
-
-        def fill(t, carry):
-            total = block(h, i, t) + br[i, t - lo].astype(F32)
+        for k, (n, t) in enumerate(half):
+            total = block(h, i, t) + br[i, n].astype(F32)
             if relayed:
-                total += xr[m - 4, t - first].astype(F32)
-            xs[m, t - first] = total.astype(BF)
-            return carry
-
-        lax.fori_loop(first, last, fill, 0)
+                total += xr[m - 4, k].astype(F32)
+            xs[m, k] = total.astype(BF)
         x_copy(p, m).start()
 
     def x_first(p):
-        block, lo, hi = parts[p]
-        mid = (lo + hi) // 2
+        block, tms = parts[p]
+        one, two = halves(p)
         br, ac = bufs[p][1], bufs[p][4]
         core_copy(p, 2).wait()
-        x_fill(p, 0, (x + 2) % 4, lo, mid, False)
-        x_fill(p, 1, (x + 2) % 4, mid, hi, False)
+        x_fill(p, 0, (x + 2) % 4, one, False)
+        x_fill(p, 1, (x + 2) % 4, two, False)
         core_copy(p, 1).wait()
-        x_fill(p, 2, (x + 1) % 4, mid, hi, False)
+        x_fill(p, 2, (x + 1) % 4, two, False)
         core_copy(p, 3).wait()
-        x_fill(p, 3, (x + 3) % 4, lo, mid, False)
+        x_fill(p, 3, (x + 3) % 4, one, False)
         core_copy(p, 0).wait()
-
-        def keep(t, carry):
-            ac[t - lo] = block(h, x, t) + br[x, t - lo].astype(F32)
-            return carry
-
-        lax.fori_loop(lo, hi, keep, 0)
+        for n, t in enumerate(tms):
+            ac[n] = block(h, x, t) + br[x, n].astype(F32)
 
     def x_second(p):
-        _, lo, hi = parts[p]
-        mid = (lo + hi) // 2
+        one, two = halves(p)
         x_copy(p, 0).wait()
-        x_fill(p, 4, (x + 1) % 4, lo, mid, True)
+        x_fill(p, 4, (x + 1) % 4, one, True)
         x_copy(p, 1).wait()
-        x_fill(p, 5, (x + 3) % 4, mid, hi, True)
-
-    def y_copy(p, t):
+        x_fill(p, 5, (x + 3) % 4, two, True)
+
+    def y_copy(p, n):
+        t = parts[p][1][n]
         ys, yr = y_bufs[p]
-        n = p * 4 + t - parts[p][1]
         return pltpu.make_async_remote_copy(
-            src_ref=ys.at[t - parts[p][1]], dst_ref=yr.at[y], send_sem=y_s.at[n],
-            recv_sem=y_r.at[p // 2 * 8 + y], device_id=(t, r, c), device_id_type=MESH)
+            src_ref=ys.at[n], dst_ref=yr.at[y], send_sem=y_s.at[p // 3 * 8 + t],
+            recv_sem=y_r.at[p // 3 * 8 + y], device_id=(t, r, c), device_id_type=MESH)
 
     def y_send(p):
-        _, lo, hi = parts[p]
-        mid = (lo + hi) // 2
-        xr, ac = bufs[p][3], bufs[p][4]
-        ys = y_bufs[p][0]
+        xr, ac, ys = bufs[p][3], bufs[p][4], y_bufs[p][0]
         for m in range(2, 6):
             x_copy(p, m).wait()
-        for first, last, one, two in ((lo, mid, 4, 3), (mid, hi, 5, 2)):
-
-            def fill(t, carry):
-                total = ac[t - lo] + xr[one, t - first].astype(F32) + xr[two, t - first].astype(F32)
-                ac[t - lo] = total
-                ys[t - lo] = total.astype(BF)
-                return carry
-
-            lax.fori_loop(first, last, fill, 0)
-        for t in range(lo, hi):
+        for half, one, two in zip(halves(p), (4, 5), (3, 2)):
+            for k, (n, t) in enumerate(half):
+                total = ac[n] + xr[one, k].astype(F32) + xr[two, k].astype(F32)
+                ac[n] = total
+                ys[n] = total.astype(BF)
+        for n, t in enumerate(parts[p][1]):
 
             @pl.when(y != t)
             def _():
-                y_copy(p, t).start()
+                y_copy(p, n).start()
 
     def y_wait_send(p):
-        _, lo, hi = parts[p]
-        for t in range(lo, hi):
+        for n, t in enumerate(parts[p][1]):
 
             @pl.when(y != t)
             def _():
-                y_copy(p, t).wait_send()
-
-    def y_sum(p):
-        _, lo, _ = parts[p]
+                y_copy(p, n).wait_send()
+
+    def y_sum(p, dst):
         ac, yr = bufs[p][4], y_bufs[p][1]
-        total = ac[y - lo]
-        for o in range(1, 8):
-            k = (y + o) % 8
-            pltpu.make_async_copy(yr.at[k], yr.at[k], y_r.at[p // 2 * 8 + k]).wait()
-            total += yr[k].astype(F32)
-        return total
-
-    lax.fori_loop(0, 5, conv_taps, 0)
+        at = 0
+        for n, t in enumerate(parts[p][1]):
+            at = jnp.where(y == t, n + 1, at)
+
+        @pl.when(at > 0)
+        def _():
+            total = ac[at - 1]
+            for o in range(1, 8):
+                k = (y + o) % 8
+                pltpu.make_async_copy(yr.at[k], yr.at[k], y_r.at[p // 3 * 8 + k]).wait()
+                total += yr[k].astype(F32)
+            dst[...] = total.reshape(dst.shape)
+
+    lax.fori_loop(0, 2, conv_taps, 0)
+    conv_tap(2, 0)
     core_send(0)
-    lax.fori_loop(5, 7, conv_taps, 0)
+    conv_tap(2, 1)
+    conv_tap(2, 2)
+    conv_taps(3, 0)
+    lax.fori_loop(4, 9, conv_taps, 0)
+    core_send(1)
+    core_send(2)
     x_first(0)
-    lax.fori_loop(7, 9, conv_taps, 0)
-    core_send(1)
+    x_first(1)
 
     def back(n, total):
         a, i = n // 3, n % 3
@@ -428,8 +428,6 @@
         return total
 
     hidden_grad = lax.fori_loop(0, 9, back, jnp.zeros((192, 192), F32))
-    x_first(1)
-    x_second(0)
     scaled_grad = hidden_grad * sigma * (1.0 + scaled * (1.0 - sigma))
     gain_local = jnp.sum(scaled_grad * normed, axis=0, keepdims=True)
     normed_grad = scaled_grad * gain
@@ -454,25 +452,21 @@
 
     g1 = small(g_core, h, gc_s, gc_r, 0, partner)
     g1.start()
+    x_first(2)
 
 
     def lift_taps(n, carry):
         for j in range(3):
             at = pl.multiple_of((n * 3 + j) * 192, 192)
-            view = slp[j, :, pl.ds(n, 4)].reshape(192, 384)
+            view = sl[j, :, pl.ds(n, 4)].reshape(192, 384)
             planes(mm_tn(view, delta), 192, fr, at)
         return carry
 
-    lax.fori_loop(0, 2, lift_taps, 0)
-    core_send(2)
-    x_second(1)
-    lax.fori_loop(2, 3, lift_taps, 0)
-    x_first(2)
+    lax.fori_loop(0, 3, lift_taps, 0)
     core_send(3)
-
+    core_send(4)
     for copy in rows_d:
         copy.wait()
-
     hs_d[...] = mm(edge_delta[...], xd[...].reshape(288, 192)).astype(BF)
     cols_d = [
         Halo(hs_d.at[pl.ds(0, 32)], rim_d.at[1], 9, 0, 0, -1),
@@ -487,20 +481,24 @@
     for copy in g2:
         copy.start()
 
+    x_second(0)
+    x_second(1)
     x_first(3)
+    x_first(4)
     x_second(2)
     y_send(0)
+    y_send(1)
     x_second(3)
-
     for copy in g2:
         copy.wait()
     g_y[y] = (g_x[0] + g_x[1]) + (g_x[2] + g_x[3])
     g3 = [small(g_y, y, gy_s, gy_r, o - 1, dev(o)) for o in range(1, 8)]
     for copy in g3:
         copy.start()
-
-    y_send(1)
+    x_second(4)
     y_send(2)
+    y_send(3)
+    y_send(4)
 
     for copy in cols_d:
         copy.wait()
@@ -521,7 +519,6 @@
     lifted_grad = lax.fori_loop(0, 3, unlift, jnp.zeros((192, 384), F32))
     gi_ref[...] = lifted_grad.reshape(3, 2, 4, 8, 384).sum(axis=2).astype(BF)
 
-    y_send(3)
 
     for copy in g3:
         copy.wait()
@@ -553,14 +550,8 @@
         def _():
             pltpu.make_async_copy(src.at[q], dst.at[z], fin_r.at[n * 8 + z]).start()
 
-    @pl.when(y < 4)
-    def _():
-        sum_c[...] = y_sum(0)
-
-    @pl.when(y >= 4)
-    def _():
-        sum_c[...] = y_sum(1)
-
+    for p in range(3):
+        y_sum(p, sum_c)
     pw_c[...] = jnp.zeros((3, 48, 128), F32)
     for q in range(3):
         pw_c[q, 0:40] = sum_c[40 * q : 40 * q + 40]
@@ -570,14 +561,8 @@
         ws_c[q] = jnp.concatenate(rows + [extra], axis=0).astype(BF)
         fin_start(0, q)
 
-    @pl.when(y < 4)
-    def _():
-        pw_r[...] = y_sum(2).reshape(3, 32, 128)
-
-    @pl.when(y >= 4)
-    def _():
-        pw_r[...] = y_sum(3).reshape(3, 32, 128)
-
+    y_sum(3, pw_r)
+    y_sum(4, pw_r)
     pack[...] = jnp.zeros((16, 128), F32)
     for q in range(8):
         low = (27 * q) // 8
@@ -612,7 +597,7 @@
 
     oc_ref[...] = cut(flat_c, 192 * (r % 2) + 24 * c)
 
-    for p in range(4):
+    for p in range(5):
         y_wait_send(p)
     for n in range(2):
         for q in range(8):
@@ -629,13 +614,8 @@
     or_ref[...] = cut(flat_r, 1296 * c - 384 * ((27 * c) // 8))
 
 
-def hand_over(gi, oc, orr, og, gi_out, oc_out, or_out, og_out, sem):
-    pairs = ((gi, gi_out), (oc, oc_out), (orr, or_out), (og, og_out))
-    copies = [pltpu.make_async_copy(a, b, sem.at[n]) for n, (a, b) in enumerate(pairs)]
-    for copy in copies:
-        copy.start()
-    for copy in copies:
-        copy.wait()
+def hand_over(gi, oc, orr, og, gi_out, oc_out, or_out, og_out):
+    gi_out[...], oc_out[...], or_out[...], og_out[...] = gi[...], oc[...], orr[...], og[...]
 
 
 def local(latent, cotangent, resample_weight, conv_weight, norm_gain):
@@ -652,20 +632,22 @@
 
     scratch = [V(a.shape, BF) for a in consts]
     scratch += [
-        V((3, 2, 8, 384), BF), V((1, 192), F32), V((3, 3, 192, 384), BF), V((3, 3, 3, 192, 192), BF),
-        V((3, 5, 6, 16, 192), BF), V((3, 4, 16, 384), BF), V((3, 4, 16, 384), BF),
+        V((3, 2, 8, 384), BF), V((1, 192), F32), V((3, 3, 192, 384), BF), V((3, 3, 192, 384), BF),
+        V((3, 3, 3, 192, 192), BF),
+        V((3, 5, 6, 16, 192), BF), V((3, 4, 16, 384), BF),
         V((192, 128), BF), V((2, 128, 128), BF), V((64, 192), BF), V((2, 32, 192), BF),
-        V((3, 3, 6, 16, 384), BF), V((3, 3, 6, 16, 384), BF),
+        V((3, 3, 6, 16, 384), BF),
         V((3, 6, 16, 192), BF), V((3, 3, 6, 16, 192), BF),
         V((3, 2592 + 48, 128), F32), V((3, 1728 + 32, 128), F32),
         V((2, 8, 128), F32), V((4, 8, 128), F32), V((8, 8, 128), F32),
         V((128, 128), F32), V((3, 48, 128), F32), V((3, 32, 128), F32),
         V((8, 32, 128), BF), V((8, 16, 128), BF), V((8, 32, 128), BF), V((8, 16, 128), BF),
         V((16, 128), F32), V((24, 128), F32), V((24, 128), F32),
-        dma((17,)), dma((23,)), dma((23,)), dma((16,)), dma((16,)), dma((24,)), dma((24,)), dma((16,)), dma((16,)),
+        dma((17,)), dma((23,)), dma((23,)), dma((20,)), dma((20,)), dma((30,)), dma((30,)), dma((16,)), dma((16,)),
         dma((16,)), dma((16,)), dma((1,)), dma((1,)), dma((3,)), dma((3,)), dma((7,)), dma((7,)),
-        *reduce_buffers(128, 4), *reduce_buffers(128, 4), *reduce_buffers(96, 4), *reduce_buffers(96, 4),
-        V((4, 128, 128), BF), V((4, 128, 128), BF), V((4, 96, 128), BF), V((4, 96, 128), BF), V((8, 128, 128), BF), V((8, 96, 128), BF),
+        *reduce_buffers(128, 2), *reduce_buffers(128, 2), *reduce_buffers(128, 4),
+        *reduce_buffers(96, 4), *reduce_buffers(96, 4),
+        V((2, 128, 128), BF), V((2, 128, 128), BF), V((4, 128, 128), BF), V((4, 96, 128), BF), V((4, 96, 128), BF), V((8, 128, 128), BF), V((8, 96, 128), BF),
     ]
     gi, oc, orr, og = pl.pallas_call(
         kernel,
@@ -685,7 +667,7 @@
     )(latent, cotangent, norm_gain.reshape(1, 192), jnp.swapaxes(resample_weight, 2, 3), conv_weight, *consts)
     shapes = [jax.ShapeDtypeStruct(a.shape, a.dtype) for a in (gi, oc, orr, og)]
     gi, oc, orr, og = pl.pallas_call(
-        hand_over, out_shape=shapes, in_specs=[far] * 4, out_specs=[far] * 4, scratch_shapes=[dma((4,))]
+        hand_over, out_shape=shapes, in_specs=[vm] * 4, out_specs=[vm] * 4
     )(gi, oc, orr, og)
     return gi, orr.reshape(-1)[:1296], oc.reshape(-1)[:1944], og.reshape(-1)[:192]
 

time: 64.2 us -> 62.3 us (0.970); the launches traced: 63.1 us -> 62 us
  Pallas kernels: 62.4 us -> 61.4 us
    pallas_call x1, Pallas kernels: 2.78 us -> 1.42 us  [local(): pl.pallas_call(hand_over, out_shape=shapes, in_specs=[vm] * 4, out_specs=...]
where the time goes in v4:
time: 62.3 us; the launch traced here: 62 us
  Pallas kernels  61.4 us (99%)
  between operations  0.64 us (1%)
    pallas_call x1, Pallas kernels, local(): pl.pallas_call(kernel, out_shape=[jax.ShapeDtypeStruct((3, 2, 8, 384), BF...  59.9 us
    pallas_call x1, Pallas kernels, local(): pl.pallas_call(hand_over, out_shape=shapes, in_specs=[vm] * 4, out_specs=...  1.42 us

profile of v4, /device:TPU:57, one launch (start us, length us, event | category | flops | bytes accessed | tf_op | source)
XLA Modules:
  0.0 62.0 jit_solution(3943407025069739945)
XLA Ops:
  0.6 59.9 %shard_map.192 = (bf16[3,2,8,384]{3,2,1,0:T(8,128)(2,1)}, f32[16,128]{1,0:T(8,128)}, f32[16,128]{1,0:T(8,128)}, f32[2,128]{1,0:T(2,128)}) custom-call(bf16[3,2,8,384]{3,2,1,0:T(8,128)(2,1)} %refs_0_.1, bf16[3,4,16,192]{3,2,1,0:T(8,128)(2,1)} %refs_1_.1, f32[1,192]{1,0:T(1,128)} %bitcast.11, bf16[3,3,192,384]{3,2,1,0:T(8,128)(2,1)} %bitcast.8, ...), custom_call_target="tpu_custom_call" | custom-call | flops 1600000000 | bytes 5000000 | tf_op jit(solution)/shard_map/pallas_call | solution.py:652
  60.6 1.4 %shard_map.193 = (bf16[3,2,8,384]{3,2,1,0:T(8,128)(2,1)}, f32[16,128]{1,0:T(8,128)}, f32[16,128]{1,0:T(8,128)}, f32[2,128]{1,0:T(2,128)}) custom-call(bf16[3,2,8,384]{3,2,1,0:T(8,128)(2,1)} %get-tuple-element.12.gi, f32[16,128]{1,0:T(8,128)} %get-tuple-element.13.oc, f32[16,128]{1,0:T(8,128)} %get-tuple-element.14.orr, f32[2,128]{1,0:T(2,128)} %get-tuple-element.15.og), custom_call_target="tpu_custom_call" | custom-call | tf_op jit(solution)/shard_map/pallas_call | solution.py:669

commit v5 on v4

--- a/solution.py
+++ b/solution.py
@@ -420,6 +420,7 @@
     core_send(2)
     x_first(0)
     x_first(1)
+    x_first(2)
 
     def back(n, total):
         a, i = n // 3, n % 3
@@ -452,7 +453,8 @@
 
     g1 = small(g_core, h, gc_s, gc_r, 0, partner)
     g1.start()
-    x_first(2)
+    x_second(0)
+    x_second(1)
 
 
     def lift_taps(n, carry):
@@ -481,8 +483,6 @@
     for copy in g2:
         copy.start()
 
-    x_second(0)
-    x_second(1)
     x_first(3)
     x_first(4)
     x_second(2)

time: 62.3 us -> 61.8 us (level)
  no operation moved by 1% of the time
where the time goes in v5:
time: 61.8 us; the launch traced here: 61.6 us
  Pallas kernels  61 us (99%)
  between operations  0.64 us (1%)
    pallas_call x1, Pallas kernels, local(): pl.pallas_call(kernel, out_shape=[jax.ShapeDtypeStruct((3, 2, 8, 384), BF...  59.6 us
    pallas_call x1, Pallas kernels, local(): pl.pallas_call(hand_over, out_shape=shapes, in_specs=[vm] * 4, out_specs=...  1.42 us

profile of v5, /device:TPU:57, one launch (start us, length us, event | category | flops | bytes accessed | tf_op | source)
XLA Modules:
  0.0 61.6 jit_solution(15024687093401395207)
XLA Ops:
  0.6 59.6 %shard_map.192 = (bf16[3,2,8,384]{3,2,1,0:T(8,128)(2,1)}, f32[16,128]{1,0:T(8,128)}, f32[16,128]{1,0:T(8,128)}, f32[2,128]{1,0:T(2,128)}) custom-call(bf16[3,2,8,384]{3,2,1,0:T(8,128)(2,1)} %refs_0_.1, bf16[3,4,16,192]{3,2,1,0:T(8,128)(2,1)} %refs_1_.1, f32[1,192]{1,0:T(1,128)} %bitcast.11, bf16[3,3,192,384]{3,2,1,0:T(8,128)(2,1)} %bitcast.8, ...), custom_call_target="tpu_custom_call" | custom-call | flops 1600000000 | bytes 5000000 | tf_op jit(solution)/shard_map/pallas_call | solution.py:652
  60.2 1.4 %shard_map.193 = (bf16[3,2,8,384]{3,2,1,0:T(8,128)(2,1)}, f32[16,128]{1,0:T(8,128)}, f32[16,128]{1,0:T(8,128)}, f32[2,128]{1,0:T(2,128)}) custom-call(bf16[3,2,8,384]{3,2,1,0:T(8,128)(2,1)} %get-tuple-element.12.gi, f32[16,128]{1,0:T(8,128)} %get-tuple-element.13.oc, f32[16,128]{1,0:T(8,128)} %get-tuple-element.14.orr, f32[2,128]{1,0:T(2,128)} %get-tuple-element.15.og), custom_call_target="tpu_custom_call" | custom-call | tf_op jit(solution)/shard_map/pallas_call | solution.py:669

commit v6 on v5

--- a/solution.py
+++ b/solution.py
@@ -484,8 +484,8 @@
         copy.start()
 
     x_first(3)
+    x_second(2)
     x_first(4)
-    x_second(2)
     y_send(0)
     y_send(1)
     x_second(3)

time: 61.8 us -> 61 us (0.987)
  Pallas kernels: 61 us -> 59.9 us
    pallas_call x1, Pallas kernels: 59.6 us -> 58.5 us  [local(): pl.pallas_call(kernel, out_shape=[jax.ShapeDtypeStruct((3, 2, 8, 384), BF...]
where the time goes in v6:
time: 61 us; the launch traced here: 60.6 us
  Pallas kernels  59.9 us (98%)
  between operations  0.64 us (1%)
    pallas_call x1, Pallas kernels, local(): pl.pallas_call(kernel, out_shape=[jax.ShapeDtypeStruct((3, 2, 8, 384), BF...  58.5 us
    pallas_call x1, Pallas kernels, local(): pl.pallas_call(hand_over, out_shape=shapes, in_specs=[vm] * 4, out_specs=...  1.42 us

profile of v6, /device:TPU:57, one launch (start us, length us, event | category | flops | bytes accessed | tf_op | source)
XLA Modules:
  0.0 60.6 jit_solution(14068439105266353237)
XLA Ops:
  0.6 58.5 %shard_map.192 = (bf16[3,2,8,384]{3,2,1,0:T(8,128)(2,1)}, f32[16,128]{1,0:T(8,128)}, f32[16,128]{1,0:T(8,128)}, f32[2,128]{1,0:T(2,128)}) custom-call(bf16[3,2,8,384]{3,2,1,0:T(8,128)(2,1)} %refs_0_.1, bf16[3,4,16,192]{3,2,1,0:T(8,128)(2,1)} %refs_1_.1, f32[1,192]{1,0:T(1,128)} %bitcast.11, bf16[3,3,192,384]{3,2,1,0:T(8,128)(2,1)} %bitcast.8, ...), custom_call_target="tpu_custom_call" | custom-call | flops 1600000000 | bytes 5000000 | tf_op jit(solution)/shard_map/pallas_call | solution.py:652
  59.1 1.4 %shard_map.193 = (bf16[3,2,8,384]{3,2,1,0:T(8,128)(2,1)}, f32[16,128]{1,0:T(8,128)}, f32[16,128]{1,0:T(8,128)}, f32[2,128]{1,0:T(2,128)}) custom-call(bf16[3,2,8,384]{3,2,1,0:T(8,128)(2,1)} %get-tuple-element.12.gi, f32[16,128]{1,0:T(8,128)} %get-tuple-element.13.oc, f32[16,128]{1,0:T(8,128)} %get-tuple-element.14.orr, f32[2,128]{1,0:T(2,128)} %get-tuple-element.15.og), custom_call_target="tpu_custom_call" | custom-call | tf_op jit(solution)/shard_map/pallas_call | solution.py:669
